TPU v7x, 128 devices: a whole 4x4x4 slice. The times are simulated.
128 devices in a mesh: dp: 16 (over x_lo, y, core), mp: 8 (over x_hi, z).
Axes of the slice: x: 4 (x_hi: 2, x_lo: 2; x = x_hi * 2 + x_lo), y: 4, z: 4, core: 2. Of those that a mesh axis runs over, the one named last changes fastest.
Arguments:
- pair_tokens: bfloat16 [256, 48, 8192], P('dp', None, 'mp'), may hold values from -6 to 6
- norm_gain: float32 [8192], replicated, may hold values from 0.1 to 1.9
- q_weight: bfloat16 [8192, 4096], P('dp', 'mp'), may hold values from -1.5 to 1.5
- k_weight: bfloat16 [8192, 1024], P('dp', 'mp'), may hold values from -1.5 to 1.5
- value_weight: bfloat16 [8192, 1024], P('dp', 'mp'), may hold values from -0.0625 to 0.0625
- o_weight: bfloat16 [4096, 8192], P('mp', 'dp'), may hold values from -0.375 to 0.375
- pair_row: int32 [256], replicated, may hold values from 0 to 63, as said below
- pair_span: int32 [256, 2], replicated, may hold values from 0 to 128, as said below
- block_ids: int32 [8192], P('dp'), may hold values from 0 to 11, as said below
Outputs:
- attn_out: bfloat16 [8192, 8192], P('dp', 'mp')
Inputs may be any that keep to these rules, and one draw needn't show every extreme that they name: `pair_row`: every packed row is tiled exactly by the spans of the pairs that name it; the pairs listed on one index of dp that name rows of one index of dp number at most 1, and 1 is reached. `pair_span`: each span holds one pair, start before end; end - start is at least 3 and at most 48; 48 is reached in every row, and the last pair of every row ends at 128. `block_ids`: the pair's place counts the pairs of its row in order of position; roles are 0 prompt, 1 chosen, 2 rejected, in that order within each pair, each present; consistent with pair_row and pair_span.
All inputs are finite; a program needn't handle non-finite values.
Results may differ from a plain program's by a relative error of at most 0.013.
Values may be sent and summed in bfloat16 or wider, within the bound.
No kernel may reach another device: no remote copies, remote signals or barrier semaphores. Data moves between devices by JAX's collectives and lax.ppermute only.
A program may use at most 128 MiB of HBM per device.

v0:
```python
import functools

import jax
import jax.numpy as jnp
from jax import lax
from jax.experimental import pallas as pl
from jax.experimental.pallas import tpu as pltpu
from jax.sharding import Mesh, PartitionSpec as P

HEAD_SIZE = 128
ROW_TOKENS = 128
QUERY_PER_KV = 4
BF = jnp.bfloat16
F32 = jnp.float32

VMEM = pl.BlockSpec(memory_space=pltpu.VMEM)
SMEM = pl.BlockSpec(memory_space=pltpu.SMEM)
ANY = pl.BlockSpec(memory_space=pl.ANY)
CHUNKS = 2
STEPS = (0, 3, 1, 2)


def params(mib):
    return pltpu.CompilerParams(vmem_limit_bytes=mib * 1024 * 1024)


def cost(flops, nbytes):
    return pl.CostEstimate(flops=flops, bytes_accessed=nbytes, transcendentals=0)


def dispatch_kernel(rows_dev, place, pair_row, pairs, out):
    count, _, width = pairs.shape
    half = width // 2
    for p in range(count):
        owner = lax.div(pair_row[place[0] * count + p], rows_dev)
        chip = lax.div(owner, 2)
        core = owner - 2 * chip
        for k in range(2):
            out[chip, k, core] = pairs[p, :, k * half : (k + 1) * half]


def dispatch(own, pair_row, pair_tokens, rows_dev):
    count, cap, width = pair_tokens.shape
    return pl.pallas_call(
        functools.partial(dispatch_kernel, rows_dev),
        in_specs=[SMEM, SMEM, VMEM],
        out_specs=VMEM,
        out_shape=jax.ShapeDtypeStruct((count // 2, 2, 2, cap, width // 2), BF),
        name="dispatch",
        compiler_params=params(60),
        cost_estimate=cost(0, 4 * count * cap * width),
    )(own.reshape(1), pair_row, pair_tokens)


def pack_kernel(target, incoming, packed):
    sources, cores, cap, width = incoming.shape
    rows = packed.shape[0] // cores
    for core in range(cores):
        slots = incoming[:, core].reshape(sources * cap, width)
        wanted = lax.broadcasted_iota(jnp.int32, (rows, sources * cap), 0)
        pick = (wanted == target[core : core + 1, :]).astype(F32).astype(BF)
        wide = jnp.dot(pick, slots, preferred_element_type=F32)
        packed[pl.ds(core * rows, rows), :] = wide.astype(BF)


def pack(target, incoming, rows):
    sources, cores, cap, width = incoming.shape
    return pl.pallas_call(
        pack_kernel,
        in_specs=[VMEM] * 2,
        out_specs=VMEM,
        out_shape=jax.ShapeDtypeStruct((rows, width), BF),
        name="pack",
        compiler_params=params(36),
        cost_estimate=cost(2 * rows * sources * cap * width, 4 * sources * cap * width),
    )(target, incoming)


def stage_kernel(*refs):
    sources, out, sems = refs[:-2], refs[-2], refs[-1]
    copies = [
        pltpu.make_async_copy(source, out.at[i], sems.at[i]) for i, source in enumerate(sources)
    ]
    for copy in copies:
        copy.start()
    for copy in copies:
        copy.wait()


def stage(sources):
    count = len(sources)
    return pl.pallas_call(
        stage_kernel,
        in_specs=[ANY] * count,
        out_specs=VMEM,
        out_shape=pltpu.VMEM((count, *sources[0].shape), BF),
        scratch_shapes=[pltpu.SemaphoreType.DMA((count,))],
        name="stage",
        compiler_params=params(16),
        cost_estimate=cost(0, 4 * count * sources[0].size),
    )(*sources)


def project_kernel(place, x, w_q, far_low, far_high, kv_first, kv_second, *refs):
    keeps, sends, squares = refs[:CHUNKS], refs[CHUNKS : 2 * CHUNKS], refs[2 * CHUNKS]
    y, core, first = place[1], place[2], place[3]
    rows = keeps[0].shape[1]
    span = rows * CHUNKS
    depth = x.shape[2]

    def split(value):
        low, high = value[:span], value[span:]
        return jnp.where(core == 0, high, low), jnp.where(core == 0, low, high)

    blocks = [lax.rem(y + step, 4) for step in STEPS]
    tile = 256
    wide = w_q.shape[3]
    for which in range(2):
        slot = first if which == 0 else 1 - first
        for begin in range(0, wide + kv_first.shape[2], tile):
            total = jnp.zeros((2 * span, tile), F32)
            for k in range(4):
                here = slice(begin, begin + tile)
                if begin >= wide:
                    piece = (kv_first, kv_second)[which][k, :, begin - wide : begin - wide + tile]
                elif k < 3:
                    piece = w_q[k, which, :, here]
                else:
                    piece = (far_low, far_high)[which][:, here]
                total += jnp.dot(x[blocks[k]], piece, preferred_element_type=F32)
            theirs, mine = split(total)
            for chunk in range(CHUNKS):
                lo = chunk * rows
                sends[chunk][slot, :, here] = theirs[lo : lo + rows].astype(BF)
                keeps[chunk][slot, :, here] = mine[lo : lo + rows]
    total = jnp.zeros((2 * span, depth), F32)
    for k in range(4):
        wide = x[k].astype(F32)
        total += wide * wide
    squares[0], squares[1] = split(jnp.sum(total, axis=1, keepdims=True))


def project(place, x, w_q, far_low, far_high, kv_first, kv_second):
    _, tokens, depth = x.shape
    span = tokens // 2
    columns = w_q.shape[3] + kv_first.shape[2]
    rows = span // CHUNKS
    results = pl.pallas_call(
        project_kernel,
        in_specs=[SMEM] + [VMEM] * 6,
        out_specs=[VMEM] * (2 * CHUNKS + 1),
        out_shape=[pltpu.VMEM((2, rows, columns), F32)] * CHUNKS
        + [jax.ShapeDtypeStruct((2, rows, columns), BF)] * CHUNKS
        + [jax.ShapeDtypeStruct((2, span, 1), F32)],
        name="project",
        compiler_params=params(24),
        cost_estimate=cost(4 * span * depth * 4 * columns * 2, 10 * 1024 * 1024),
    )(place, x, w_q, far_low, far_high, kv_first, kv_second)
    return results[:CHUNKS], results[CHUNKS : 2 * CHUNKS], results[2 * CHUNKS]


def tables_kernel(turns, bias, out):
    out[0] = turns[...]
    out[1] = bias[...]


def tables(turns, bias):
    return pl.pallas_call(
        tables_kernel,
        in_specs=[VMEM] * 2,
        out_specs=VMEM,
        out_shape=pltpu.VMEM((2, *turns.shape), F32),
        name="tables",
        compiler_params=params(16),
        cost_estimate=cost(0, 16 * turns.size),
    )(turns, bias)


def attend_kernel(chunk, keep, near, across, squares, table, out):
    tokens = out.shape[0]
    heads = out.shape[1] // HEAD_SIZE
    width = heads * HEAD_SIZE
    lane = lax.broadcasted_iota(jnp.int32, (ROW_TOKENS, HEAD_SIZE), 1)
    low = lane < HEAD_SIZE // 2
    diagonal = lane == lax.broadcasted_iota(jnp.int32, (ROW_TOKENS, HEAD_SIZE), 0)
    for r in range(tokens // ROW_TOKENS):
        here = slice(r * ROW_TOKENS, (r + 1) * ROW_TOKENS)
        row = chunk * (tokens // ROW_TOKENS) + r
        there = slice(row * ROW_TOKENS, (row + 1) * ROW_TOKENS)
        column = jnp.sum(jnp.where(diagonal, squares[row : row + 1, :], 0.0), axis=1, keepdims=True)
        scale = lax.rsqrt(column + 1e-05)
        both = keep[0, here, :] + near[0, here, :].astype(F32) + across[here, :].astype(F32)
        both = both * scale
        turn = table[0, there, :]
        turned = pltpu.roll(turn, HEAD_SIZE // 2, 1)
        cos = jnp.where(low, turn, turned)
        sin = jnp.where(low, -turned, turn)

        def rotate(u):
            return (u * cos + pltpu.roll(u, HEAD_SIZE // 2, 1) * sin).astype(BF)

        key = rotate(both[:, width : width + HEAD_SIZE])
        value = both[:, width + HEAD_SIZE :].astype(BF)
        query = jnp.concatenate(
            [rotate(both[:, h * HEAD_SIZE : (h + 1) * HEAD_SIZE]) for h in range(heads)], axis=0
        )
        scores = lax.dot_general(
            query, key, (((1,), (1,)), ((), ())), preferred_element_type=F32
        ) * HEAD_SIZE ** (-0.5)
        scores = scores + jnp.concatenate([table[1, there, :]] * heads, axis=0)
        top = jnp.max(scores, axis=-1, keepdims=True)
        expo = jnp.exp(scores - top)
        probs = (expo / jnp.sum(expo, axis=-1, keepdims=True)).astype(BF)
        result = jnp.dot(probs, value, preferred_element_type=F32).astype(BF)
        for h in range(heads):
            out[here, h * HEAD_SIZE : (h + 1) * HEAD_SIZE] = result[
                h * ROW_TOKENS : (h + 1) * ROW_TOKENS
            ]


def attend(chunk, keep, near, across, squares, table):
    _, tokens, columns = keep.shape
    width = columns - 2 * HEAD_SIZE
    return pl.pallas_call(
        functools.partial(attend_kernel, chunk),
        in_specs=[VMEM] * 5,
        out_specs=VMEM,
        out_shape=jax.ShapeDtypeStruct((tokens, width), BF),
        name="attend",
        compiler_params=params(16),
        cost_estimate=cost(4 * tokens * width * ROW_TOKENS, 8 * tokens * columns),
    )(keep, near, across, squares, table)


def expand_kernel(steps, place, *refs):
    pairs, weights, outs = (refs[0:2], refs[2:4]), refs[4], refs[5:]
    z, first = place[0], place[3]
    straight = first == 0
    wide = weights.shape[-1]
    outs = iter(outs)
    for (mine, other), chosen in zip(pairs, steps):
        left = jnp.where(straight, mine[...], other[...])
        right = jnp.where(straight, other[...], mine[...])
        for step in chosen:
            out = next(outs)
            block = 2 * lax.rem(z + step, 4)
            for k in range(2):
                total = jnp.dot(left, weights[block + k, 0], preferred_element_type=F32)
                total += jnp.dot(right, weights[block + k, 1], preferred_element_type=F32)
                out[:, k * wide : (k + 1) * wide] = total.astype(BF)


def expand(steps, place, attns, swapped, weights):
    tokens, depth = attns[0].shape
    wide = weights.shape[-1]
    count = sum(len(chosen) for chosen in steps)
    return pl.pallas_call(
        functools.partial(expand_kernel, steps),
        in_specs=[SMEM] + [VMEM] * 5,
        out_specs=[VMEM] * count,
        out_shape=[jax.ShapeDtypeStruct((tokens, 2 * wide), BF)] * count,
        name="expand",
        compiler_params=params(16),
        cost_estimate=cost(count * 8 * tokens * depth * wide, count * 3 * 1024 * 1024),
    )(place, attns[0], swapped[0], attns[1], swapped[1], weights)


def after(values, *events):
    return lax.optimization_barrier((*values, *events))


def shift(x, axis, by):
    size = lax.axis_size(axis)
    return lax.ppermute(x, axis, [(i, (i + by) % size) for i in range(size)])


def spread(x):
    def at(place):
        return (place % 2) * 2 + place // 2

    first = [(0, 1), (1, 3), (2, 0), (3, 2)]
    second = [(0, 0), (1, 2), (2, 1), (3, 3)]
    return tuple(
        lax.ppermute(x, ("xl", "xh"), [(at(a), at(b)) for a, b in pairs])
        for pairs in (first, second)
    )


def row_mask(ids):
    pair_of = ids // 3
    role_of = ids % 3
    steps_a = jnp.arange(ids.shape[0])
    causal = steps_a[None, :] <= steps_a[:, None]
    same = pair_of[:, None] == pair_of[None, :]
    hidden_pair = (role_of[:, None] == 2) & (role_of[None, :] == 1)
    return causal & same & jnp.logical_not(hidden_pair)


def local(
    pair_tokens,
    norm_gain,
    q_weight,
    k_weight,
    value_weight,
    o_weight,
    pair_row,
    pair_span,
    block_ids,
):
    dp = ("xl", "y", "c")
    dp_count = lax.axis_size(dp)
    own = lax.axis_index(dp)
    xl, y, core = (lax.axis_index(a) for a in dp)
    xh, z = lax.axis_index("xh"), lax.axis_index("z")
    pairs_dev, pair_cap, width_local = pair_tokens.shape
    tok_dev = block_ids.shape[0]
    rows_dev = tok_dev // ROW_TOKENS
    first = jnp.where(xh == 1 - xl, 0, 1).astype(jnp.int32)

    owners_all = (pair_row // rows_dev).reshape(dp_count, pairs_dev)
    rows = q_weight.shape[0]
    gain = lax.dynamic_slice_in_dim(norm_gain, own * rows, rows, 0)[:, None]
    q_in = (q_weight.astype(F32) * gain).astype(BF)
    kv_in = jnp.concatenate([k_weight, value_weight], axis=1)
    kv_in = (kv_in.astype(F32) * gain).astype(BF)
    outgoing = dispatch(own.astype(jnp.int32), pair_row, pair_tokens, rows_dev)
    q_pair = spread(q_in)
    kv_blocks = (kv_in, shift(kv_in, "y", 1), shift(kv_in, "y", -1), shift(kv_in, "y", 2))
    outgoing = outgoing.reshape(dp_count, 2, pair_cap, width_local // 2)
    incoming = lax.all_to_all(outgoing, dp, split_axis=0, concat_axis=0, tiled=True)

    incoming = after((incoming,), *q_pair, *kv_blocks)[0]

    slots = jnp.arange(pair_cap, dtype=jnp.int32)
    begin = ((pair_row % rows_dev) * ROW_TOKENS + pair_span[:, 0]).reshape(dp_count, pairs_dev)
    length = (pair_span[:, 1] - pair_span[:, 0]).reshape(dp_count, pairs_dev)
    owner_here = (own // 2) * 2 + jnp.arange(2, dtype=jnp.int32)
    match = owners_all[None] == owner_here[:, None, None]
    begin_here = jnp.sum(jnp.where(match, begin[None], 0), axis=2)
    length_here = jnp.sum(jnp.where(match, length[None], 0), axis=2)
    target = jnp.where(
        slots[None, None, :] < length_here[:, :, None],
        begin_here[:, :, None] + slots[None, None, :],
        -1,
    ).reshape(2, dp_count * pair_cap)
    packed = pack(target, incoming, 2 * tok_dev)
    x_blocks = lax.all_gather(packed, "z", axis=0, tiled=False)

    q_both = jnp.stack(after(q_pair, packed)[:2])
    q_before, q_behind = shift(q_both, "y", 1), shift(q_both, "y", -1)
    kv_all = jnp.stack(after(kv_blocks, packed)[:4])
    kv_first, kv_second = spread(kv_all)
    q_from, q_back = after((q_before, q_behind), kv_first, kv_second)[:2]
    far_low, far_high = shift(q_from[0], "y", 1), shift(q_back[1], "y", -1)
    w_q = stage((q_both, q_before, q_behind))

    visible = jax.vmap(row_mask)(block_ids.reshape(rows_dev, ROW_TOKENS))
    position = (jnp.sum(visible.astype(jnp.int32), axis=2) - 1).reshape(tok_dev)
    half = HEAD_SIZE // 2
    freq = 500000.0 ** (-(jnp.arange(half, dtype=F32) * 2.0 / HEAD_SIZE))
    angle = position.astype(F32)[:, None] * freq[None, :]
    turns = jnp.concatenate([jnp.cos(angle), jnp.sin(angle)], axis=1)

    bias = jnp.where(visible, 0.0, -1e30).astype(F32).reshape(tok_dev, ROW_TOKENS)

    table = tables(turns, bias)

    o_in = after((o_weight,), q_from, q_back, table)[0]
    o_pair = after(spread(o_in), far_low, far_high)[:2]
    o_both = after((jnp.stack(o_pair),), x_blocks)[0]
    o_all = lax.all_gather(o_both, ("y", "c"), axis=0, tiled=False)

    place = jnp.stack([z, y, core, first]).astype(jnp.int32)
    place, table, w_q = lax.optimization_barrier((place, table, w_q))

    keeps, sends, squares = project(place, x_blocks, w_q, far_low, far_high, kv_first, kv_second)
    squares = squares.reshape(2, tok_dev // 128, 128)
    across_both = lax.ppermute(squares[0], ("c", "xh"), [(i, 3 - i) for i in range(4)])
    squares = (
        squares[1] + shift(squares[0], "c", 1) + shift(squares[1], "xh", 1) + across_both
    )
    nears = [shift(send, "c", 1) for send in sends]
    others = [(keep[1] + near[1].astype(F32)).astype(BF) for keep, near in zip(keeps, nears)]
    across_low = shift(others[0], "xh", 1)
    across_high = shift(after((others[1],), squares)[0], "xh", 1)
    acrosses = [across_low, across_high]
    mean = squares * (1.0 / norm_gain.shape[0])
    attns = [
        attend(chunk, keeps[chunk], nears[chunk], acrosses[chunk], mean, table)
        for chunk in range(CHUNKS)
    ]
    swapped = [shift(attn, "xh", 1) for attn in attns]
    o_all = after((o_all,), *swapped)[0]

    far_low, far_high = expand(((2,), (2,)), place, attns, swapped, o_all)
    passing_low = shift(far_low, "z", 1)
    passing_high = shift(far_high, "z", -1)
    o_late = after((o_all,), far_low, far_high)[0]
    down_low, up_low, own_low, up_high, down_high, own_high = expand(
        ((3, 1, 0), (1, 3, 0)), place, attns, swapped, o_late
    )
    down_low = shift(down_low, "z", -1)
    up_high = shift(up_high, "z", 1)
    up_low = shift((up_low.astype(F32) + passing_low.astype(F32)).astype(BF), "z", 1)
    down_high = shift((down_high.astype(F32) + passing_high.astype(F32)).astype(BF), "z", -1)
    low = own_low.astype(F32) + up_low.astype(F32) + down_low.astype(F32)
    high = own_high.astype(F32) + up_high.astype(F32) + down_high.astype(F32)
    return jnp.concatenate([low.astype(BF), high.astype(BF)], axis=0)


def solution(mesh):
    fine = Mesh(mesh.devices.reshape(2, 4, 2, 2, 4), ("xl", "y", "c", "xh", "z"))
    dp, mp = ("xl", "y", "c"), ("xh", "z")
    placed = (
        P(dp, None, mp),
        P(),
        P(dp, mp),
        P(dp, mp),
        P(dp, mp),
        P(mp, dp),
        P(),
        P(),
        P(dp),
    )
    return jax.shard_map(
        local, mesh=fine, in_specs=placed, out_specs=P(dp, mp), check_vma=False
    )
```

profile of v0, /device:TPU:1, one launch (start us, length us, event | category | flops | bytes accessed | tf_op | source)
XLA Modules:
  0.0 205.5 jit_solution(7932809571836297302)
XLA Ops:
  6.5 2.8 %dispatch.1 = bf16[8,2,2,48,512]{4,3,2,1,0:T(8,128)(2,1)} custom-call(s32[1]{0:T(128)} %bitcast.12.place, s32[256]{0:T(256)} %pair_row.1, bf16[16,48,1024]{2,1,0:T(8,128)(2,1)} %pairs.1), custom_call_target="tpu_custom_call" | custom-call | bytes 3145728 | tf_op jit(solution)/shard_map/dispatch/pallas_call | solution.py:44
  9.3 7.0 %all-to-all-start = ((bf16[16,2,48,512]{3,2,1,0:T(8,128)(2,1)}), bf16[16,2,48,512]{3,2,1,0:T(8,128)(2,1)S(1)}, u32[]{:S(2)}, u32[]{:S(2)}) async-start(bf16[16,2,48,512]{3,2,1,0:T(8,128)(2,1)} %bitcast.72), calls=%async_computation | async-start | bytes 3145728 | tf_op jit(solution)/shard_map/all_to_all | solution.py:330
  16.5 0.8 dynamic_slice.3
  17.4 1.5 collective-permute-start
  18.9 1.4 collective-permute-start.1
  20.3 1.0 multiply_convert_fusion.1
  21.3 1.3 collective-permute-start.2
  22.6 1.5 collective-permute-start.3
  24.1 1.5 collective-permute-start.4
  26.5 16.1 %collective-permute-done.2 = bf16[512,256]{1,0:T(8,128)(2,1)S(1)} collective-permute-done((bf16[512,256]{1,0:T(8,128)(2,1)S(1)}, bf16[512,256]{1,0:T(8,128)(2,1)S(1)}, u32[]{:S(2)}, u32[]{:S(2)}) %collective-permute-start.2) | collective-permute-done | bytes 262176 | tf_op jit(solution)/shard_map/ppermute | solution.py:274
  42.6 5.9 %collective-permute-done.4 = bf16[512,256]{1,0:T(8,128)(2,1)} collective-permute-done((bf16[512,256]{1,0:T(8,128)(2,1)S(1)}, bf16[512,256]{1,0:T(8,128)(2,1)}, u32[]{:S(2)}, u32[]{:S(2)}) %collective-permute-start.4) | collective-permute-done | bytes 262176 | tf_op jit(solution)/shard_map/ppermute | solution.py:274
  48.5 2.0 pack.1
  50.6 1.1 pad_maximum_fusion.refs_0_
  51.8 3.1 %collective-permute-start.5 = (bf16[2,512,512]{2,1,0:T(8,128)(2,1)S(1)}, bf16[2,512,512]{2,1,0:T(8,128)(2,1)S(1)}, u32[]{:S(2)}, u32[]{:S(2)}) collective-permute-start(bf16[2,512,512]{2,1,0:T(8,128)(2,1)S(1)} %pad_maximum_fusion.refs_0_), channel_id=1, source_target_pairs={{0,16},{16,32},{32,48},{48,0},{1,17},{17,33},{33,49},{49,1},{2,18}... | collective-permute-start | bytes 3145736 | tf_op jit(solution)/shard_map/ppermute | solution.py:274
  54.8 1.2 pad_maximum_fusion.1
  56.0 1.4 collective-permute-start.7
  57.4 0.7 collective-permute-start.8
  58.1 0.3 convert_reduce_fusion
  58.5 1.0 multiply_cosine_fusion
  59.8 17.2 %collective-permute-done.5.refs_1_ = bf16[2,512,512]{2,1,0:T(8,128)(2,1)S(1)} collective-permute-done((bf16[2,512,512]{2,1,0:T(8,128)(2,1)S(1)}, bf16[2,512,512]{2,1,0:T(8,128)(2,1)S(1)}, u32[]{:S(2)}, u32[]{:S(2)}) %collective-permute-start.5) | collective-permute-done | bytes 1048608 | tf_op jit(solution)/shard_map/ppermute | solution.py:274
  77.0 1.5 collective-permute-done.6.refs_2_
  78.4 2.6 %collective-permute-done.7.kv_first = bf16[4,512,256]{2,1,0:T(8,128)(2,1)S(1)} collective-permute-done((bf16[4,512,256]{2,1,0:T(8,128)(2,1)S(1)}, bf16[4,512,256]{2,1,0:T(8,128)(2,1)S(1)}, u32[]{:S(2)}, u32[]{:S(2)}) %collective-permute-start.7) | collective-permute-done | bytes 1048608 | tf_op jit(solution)/shard_map/ppermute | solution.py:284
  81.1 1.0 copy-done.6
  82.1 1.3 collective-permute-start.9
  83.4 1.6 collective-permute-start.10
  85.0 3.4 %collective-permute-start.20 = (bf16[512,512]{1,0:T(8,128)(2,1)S(1)}, bf16[512,512]{1,0:T(8,128)(2,1)S(1)}, u32[]{:S(2)}, u32[]{:S(2)}) collective-permute-start(bf16[512,512]{1,0:T(8,128)(2,1)S(1)} %copy-done.17), channel_id=1, source_target_pairs={{0,64},{64,68},{4,0},{68,4},{1,65},{65,69},{5,1},{69,5},{2,66},{66... | collective-permute-start | bytes 1572872 | tf_op jit(solution)/shard_map/ppermute | solution.py:284
  88.4 0.9 collective-permute-start.21
  89.3 5.5 %collective-permute-done.9.far_low = bf16[512,512]{1,0:T(8,128)(2,1)S(1)} collective-permute-done((bf16[512,512]{1,0:T(8,128)(2,1)S(1)}, bf16[512,512]{1,0:T(8,128)(2,1)S(1)}, u32[]{:S(2)}, u32[]{:S(2)}) %collective-permute-start.9) | collective-permute-done | bytes 524320 | tf_op jit(solution)/shard_map/ppermute | solution.py:274
  94.8 0.8 copy-done.8
  95.6 3.3 %collective-permute-done.20 = bf16[512,512]{1,0:T(8,128)(2,1)S(1)} collective-permute-done((bf16[512,512]{1,0:T(8,128)(2,1)S(1)}, bf16[512,512]{1,0:T(8,128)(2,1)S(1)}, u32[]{:S(2)}, u32[]{:S(2)}) %collective-permute-start.20) | collective-permute-done | bytes 524320 | tf_op jit(solution)/shard_map/ppermute | solution.py:284
  98.9 1.1 pad_maximum_fusion.2
  100.0 0.6 all-gather.5.cloned.1.call-done
  100.8 1.2 copy-done.2
  102.2 1.9 copy-done.3
  104.2 0.3 copy-done.5
  104.5 0.3 copy-done.7
  104.8 1.0 copy-done.9
  105.8 7.9 %project.1 = (f32[2,256,768]{2,1,0:T(8,128)S(1)}, f32[2,256,768]{2,1,0:T(8,128)S(1)}, bf16[2,256,768]{2,1,0:T(8,128)(2,1)S(1)}, bf16[2,256,768]{2,1,0:T(8,128)(2,1)S(1)}, f32[2,512,1]{2,1,0:T(8,128)S(1)}) custom-call(s32[4]{0:T(128)S(1)} %pad_add_fusion.place, bf16[4,1024,512]{2,1,0:T(8,128)(2,1)S(1)} %bitcast.71, bf16[3,2,512,512]{3,2,1,0:T(8,128)(2,1)S(1)} %stage.1.w_q, ...), custom_call_target="tpu_custom_call" | custom-call | flops 6442450944 | bytes 10485760 | tf_op jit(solution)/shard_map/project/pallas_call | solution.py:148
  113.7 2.4 %collective-permute-start.11 = (bf16[2,256,768]{2,1,0:T(8,128)(2,1)S(1)}, bf16[2,256,768]{2,1,0:T(8,128)(2,1)S(1)}, u32[]{:S(2)}, u32[]{:S(2)}) collective-permute-start(bf16[2,256,768]{2,1,0:T(8,128)(2,1)S(1)} %get-tuple-element.49), channel_id=1, source_target_pairs={{0,8},{8,0},{1,9},{9,1},{2,10},{10,2},{3,11},{11,3},{4,12},{12,4},... | collective-permute-start | bytes 2359304 | tf_op jit(solution)/shard_map/ppermute | solution.py:274
  116.4 3.7 %collective-permute-start.15 = (f32[4,128]{1,0:T(4,128)S(1)}, f32[4,128]{1,0:T(4,128)S(1)}, u32[]{:S(2)}, u32[]{:S(2)}) collective-permute-start(f32[4,128]{1,0:T(4,128)S(1)} %bitcast.80), channel_id=1, source_target_pairs={{0,12},{4,8},{8,4},{12,0},{1,13},{5,9},{9,5},{13,1},{2,14},{6,10},... | collective-permute-start | bytes 6152 | tf_op jit(solution)/shard_map/ppermute | solution.py:378
  120.2 0.5 collective-permute-start.13
  120.7 0.8 collective-permute-done.15
  121.5 2.7 %collective-permute-done.14 = f32[4,128]{1,0:T(4,128)S(1)} collective-permute-done((f32[4,128]{1,0:T(4,128)S(1)}, f32[4,128]{1,0:T(4,128)S(1)}, u32[]{:S(2)}, u32[]{:S(2)}) %collective-permute-start.14) | collective-permute-done | bytes 2080 | tf_op jit(solution)/shard_map/ppermute | solution.py:274
  124.3 0.7 collective-permute-start.12
  125.1 2.4 %collective-permute-start.18 = (bf16[256,768]{1,0:T(8,128)(2,1)S(1)}, bf16[256,768]{1,0:T(8,128)(2,1)S(1)}, u32[]{:S(2)}, u32[]{:S(2)}) collective-permute-start(bf16[256,768]{1,0:T(8,128)(2,1)S(1)} %fusion.1), channel_id=1, source_target_pairs={{0,4},{4,0},{1,5},{5,1},{2,6},{6,2},{3,7},{7,3},{8,12},{12,8},{9,1... | collective-permute-start | bytes 1179656 | tf_op jit(solution)/shard_map/ppermute | solution.py:274
  127.5 7.8 %collective-permute-done.12.across = bf16[256,768]{1,0:T(8,128)(2,1)S(1)} collective-permute-done((bf16[256,768]{1,0:T(8,128)(2,1)S(1)}, bf16[256,768]{1,0:T(8,128)(2,1)S(1)}, u32[]{:S(2)}, u32[]{:S(2)}) %collective-permute-start.12) | collective-permute-done | bytes 393248 | tf_op jit(solution)/shard_map/ppermute | solution.py:274
  135.3 1.1 attend.2.refs_0_
  136.4 1.4 collective-permute-start.16
  137.7 6.0 %collective-permute-done.18.across = bf16[256,768]{1,0:T(8,128)(2,1)S(1)} collective-permute-done((bf16[256,768]{1,0:T(8,128)(2,1)S(1)}, bf16[256,768]{1,0:T(8,128)(2,1)S(1)}, u32[]{:S(2)}, u32[]{:S(2)}) %collective-permute-start.18) | collective-permute-done | bytes 393248 | tf_op jit(solution)/shard_map/ppermute | solution.py:274
  143.7 1.1 attend.3.refs_2_
  144.8 1.4 collective-permute-start.19
  146.1 3.2 %collective-permute-done.16.refs_1_ = bf16[256,512]{1,0:T(8,128)(2,1)S(1)} collective-permute-done((bf16[256,512]{1,0:T(8,128)(2,1)S(1)}, bf16[256,512]{1,0:T(8,128)(2,1)S(1)}, u32[]{:S(2)}, u32[]{:S(2)}) %collective-permute-start.16) | collective-permute-done | bytes 262176 | tf_op jit(solution)/shard_map/ppermute | solution.py:274
  149.3 5.0 %collective-permute-done.19.refs_3_ = bf16[256,512]{1,0:T(8,128)(2,1)S(1)} collective-permute-done((bf16[256,512]{1,0:T(8,128)(2,1)S(1)}, bf16[256,512]{1,0:T(8,128)(2,1)S(1)}, u32[]{:S(2)}, u32[]{:S(2)}) %collective-permute-start.19) | collective-permute-done | bytes 262176 | tf_op jit(solution)/shard_map/ppermute | solution.py:274
  154.3 3.4 %copy-done = bf16[16,512,512]{2,1,0:T(8,128)(2,1)S(1)} copy-done((bf16[16,512,512]{2,1,0:T(8,128)(2,1)S(1)}, bf16[16,512,512]{2,1,0:T(8,128)(2,1)}, u32[]{:S(2)}) %copy-start) | copy-done | bytes 8388632
  157.7 1.8 expand.2
  159.5 3.8 %collective-permute-start.26 = (bf16[256,1024]{1,0:T(8,128)(2,1)S(1)}, bf16[256,1024]{1,0:T(8,128)(2,1)S(1)}, u32[]{:S(2)}, u32[]{:S(2)}) collective-permute-start(bf16[256,1024]{1,0:T(8,128)(2,1)S(1)} %get-tuple-element.61), channel_id=1, source_target_pairs={{0,3},{1,0},{2,1},{3,2},{4,7},{5,4},{6,5},{7,6},{8,11},{9,8},{10,9... | collective-permute-start | bytes 1572872 | tf_op jit(solution)/shard_map/ppermute | solution.py:274
  163.3 4.0 %expand.3 = (bf16[256,1024]{1,0:T(8,128)(2,1)S(1)}, bf16[256,1024]{1,0:T(8,128)(2,1)S(1)}, bf16[256,1024]{1,0:T(8,128)(2,1)S(1)}, bf16[256,1024]{1,0:T(8,128)(2,...) custom-call(s32[4]{0:T(128)S(1)} %pad_add_fusion.place, bf16[256,512]{1,0:T(8,128)(2,1)S(1)} %attend.2.refs_0_, ...), custom_call_target="tpu_custom_call" | custom-call | flops 3221225472 | bytes 18874368 | tf_op jit(solution)/shard_map/expand/pallas_call | solution.py:257
  167.4 4.4 %collective-permute-done.26 = bf16[256,1024]{1,0:T(8,128)(2,1)S(1)} collective-permute-done((bf16[256,1024]{1,0:T(8,128)(2,1)S(1)}, bf16[256,1024]{1,0:T(8,128)(2,1)S(1)}, u32[]{:S(2)}, u32[]{:S(2)}) %collective-permute-start.26) | collective-permute-done | bytes 524320 | tf_op jit(solution)/shard_map/ppermute | solution.py:274
  171.9 3.5 %collective-permute-start.27 = (bf16[256,1024]{1,0:T(8,128)(2,1)S(1)}, bf16[256,1024]{1,0:T(8,128)(2,1)S(1)}, u32[]{:S(2)}, u32[]{:S(2)}) collective-permute-start(bf16[256,1024]{1,0:T(8,128)(2,1)S(1)} %add_convert_fusion.1), channel_id=1, source_target_pairs={{0,3},{1,0},{2,1},{3,2},{4,7},{5,4},{6,5},{7,6},{8,11},{9,8},{10,9... | collective-permute-start | bytes 1572872 | tf_op jit(solution)/shard_map/ppermute | solution.py:274
  175.7 1.5 collective-permute-start.23
  177.2 9.0 %collective-permute-done.25 = bf16[256,1024]{1,0:T(8,128)(2,1)S(1)} collective-permute-done((bf16[256,1024]{1,0:T(8,128)(2,1)S(1)}, bf16[256,1024]{1,0:T(8,128)(2,1)S(1)}, u32[]{:S(2)}, u32[]{:S(2)}) %collective-permute-start.25) | collective-permute-done | bytes 524320 | tf_op jit(solution)/shard_map/ppermute | solution.py:274
  186.4 7.8 %collective-permute-done.24 = bf16[256,1024]{1,0:T(8,128)(2,1)S(1)} collective-permute-done((bf16[256,1024]{1,0:T(8,128)(2,1)S(1)}, bf16[256,1024]{1,0:T(8,128)(2,1)S(1)}, u32[]{:S(2)}, u32[]{:S(2)}) %collective-permute-start.24) | collective-permute-done | bytes 524320 | tf_op jit(solution)/shard_map/ppermute | solution.py:274
  194.2 3.2 %collective-permute-done.23 = bf16[256,1024]{1,0:T(8,128)(2,1)S(1)} collective-permute-done((bf16[256,1024]{1,0:T(8,128)(2,1)S(1)}, bf16[256,1024]{1,0:T(8,128)(2,1)S(1)}, u32[]{:S(2)}, u32[]{:S(2)}) %collective-permute-start.23) | collective-permute-done | bytes 524320 | tf_op jit(solution)/shard_map/ppermute | solution.py:274
  197.6 1.0 pad_maximum_fusion.3
  (87 shorter events, 3.6 us)
Async XLA Ops:
  9.3 7.9 %copy-start.10 = (bf16[512,512]{1,0:T(8,128)(2,1)S(1)}, bf16[512,512]{1,0:T(8,128)(2,1)}, u32[]{:S(2)}) copy-start(bf16[512,512]{1,0:T(8,128)(2,1)} %param.11) | copy-start | bytes 1572868
  9.3 11.0 %copy-start.13 = (bf16[512,128]{1,0:T(8,128)(2,1)S(1)}, bf16[512,128]{1,0:T(8,128)(2,1)}, u32[]{:S(2)}) copy-start(bf16[512,128]{1,0:T(8,128)(2,1)} %param.13) | copy-start | bytes 393220
  9.3 39.2 %all-to-all-start = ((bf16[16,2,48,512]{3,2,1,0:T(8,128)(2,1)}), bf16[16,2,48,512]{3,2,1,0:T(8,128)(2,1)S(1)}, u32[]{:S(2)}, u32[]{:S(2)}) async-start(bf16[16,2,48,512]{3,2,1,0:T(8,128)(2,1)} %bitcast.72), calls=%async_computation | async-start | bytes 3145728 | tf_op jit(solution)/shard_map/all_to_all | solution.py:330
  16.4 9.2 %copy-start.16 = (s32[256,2]{0,1:T(2,128)S(1)}, s32[256,2]{0,1:T(2,128)}, u32[]{:S(2)}) copy-start(s32[256,2]{0,1:T(2,128)} %param.16) | copy-start | bytes 6148
  16.4 9.2 %copy-start.15 = (s32[256]{0:T(256)S(1)}, s32[256]{0:T(256)}, u32[]{:S(2)}) copy-start(s32[256]{0:T(256)} %pair_row.1) | copy-start | bytes 3076
  16.4 84.2 %all-gather.5.cloned.1.call-start = ((), (), s32[]{:S(2)}) async-start(), calls=%async_computation.1 | async-start | bytes 5242880 | tf_op jit(solution)/shard_map/all_gather | solution.py:347
  17.4 31.1 %collective-permute-start = (bf16[512,512]{1,0:T(8,128)(2,1)S(1)}, bf16[512,512]{1,0:T(8,128)(2,1)S(1)}, u32[]{:S(2)}, u32[]{:S(2)}) collective-permute-start(bf16[512,512]{1,0:T(8,128)(2,1)S(1)} %multiply_convert_fusion), channel_id=1, source_target_pairs={{0,64},{64,68},{4,0},{68,4},{1,65},{65,69},{5,1},{69,5},{2,66},{66... | collective-permute-start | bytes 1572872 | tf_op jit(solution)/shard_map/ppermute | solution.py:284
  18.9 29.6 %collective-permute-start.1 = (bf16[512,512]{1,0:T(8,128)(2,1)S(1)}, bf16[512,512]{1,0:T(8,128)(2,1)}, u32[]{:S(2)}, u32[]{:S(2)}) collective-permute-start(bf16[512,512]{1,0:T(8,128)(2,1)S(1)} %multiply_convert_fusion), channel_id=1, source_target_pairs={{0,0},{64,4},{4,64},{68,68},{1,1},{65,5},{5,65},{69,69},{2,2},{66,... | collective-permute-start | bytes 1572872 | tf_op jit(solution)/shard_map/ppermute | solution.py:284
  21.3 21.2 %collective-permute-start.2 = (bf16[512,256]{1,0:T(8,128)(2,1)S(1)}, bf16[512,256]{1,0:T(8,128)(2,1)S(1)}, u32[]{:S(2)}, u32[]{:S(2)}) collective-permute-start(bf16[512,256]{1,0:T(8,128)(2,1)S(1)} %multiply_convert_fusion.1), channel_id=1, source_target_pairs={{0,16},{16,32},{32,48},{48,0},{1,17},{17,33},{33,49},{49,1},{2,18}... | collective-permute-start | bytes 786440 | tf_op jit(solution)/shard_map/ppermute | solution.py:274
  22.6 20.0 %collective-permute-start.3 = (bf16[512,256]{1,0:T(8,128)(2,1)S(1)}, bf16[512,256]{1,0:T(8,128)(2,1)}, u32[]{:S(2)}, u32[]{:S(2)}) collective-permute-start(bf16[512,256]{1,0:T(8,128)(2,1)S(1)} %multiply_convert_fusion.1), channel_id=1, source_target_pairs={{0,48},{16,0},{32,16},{48,32},{1,49},{17,1},{33,17},{49,33},{2,50}... | collective-permute-start | bytes 786440 | tf_op jit(solution)/shard_map/ppermute | solution.py:274
  24.1 24.4 %collective-permute-start.4 = (bf16[512,256]{1,0:T(8,128)(2,1)S(1)}, bf16[512,256]{1,0:T(8,128)(2,1)}, u32[]{:S(2)}, u32[]{:S(2)}) collective-permute-start(bf16[512,256]{1,0:T(8,128)(2,1)S(1)} %multiply_convert_fusion.1), channel_id=1, source_target_pairs={{0,32},{16,48},{32,0},{48,16},{1,33},{17,49},{33,1},{49,17},{2,34}... | collective-permute-start | bytes 786440 | tf_op jit(solution)/shard_map/ppermute | solution.py:274
  26.5 24.1 %copy-start.14 = (s32[512]{0:T(512)S(1)}, s32[512]{0:T(512)}, u32[]{:S(2)}) copy-start(s32[512]{0:T(512)} %param.17) | copy-start | bytes 6148
  42.6 7.9 %copy-start.11 = (bf16[512,256]{1,0:T(8,128)(2,1)}, bf16[512,256]{1,0:T(8,128)(2,1)S(1)}, u32[]{:S(2)}) copy-start(bf16[512,256]{1,0:T(8,128)(2,1)S(1)} %collective-permute-done.2) | copy-start | bytes 786436
  50.5 103.8 %all-gather.7.cloned.1.call-start = ((), (), s32[]{:S(2)}) async-start(), calls=%async_computation.2 | async-start | bytes 9437184 | tf_op jit(solution)/shard_map/all_gather | solution.py:371
  50.5 4.3 %copy-start.12 = (bf16[512,256]{1,0:T(8,128)(2,1)S(1)}, bf16[512,256]{1,0:T(8,128)(2,1)}, u32[]{:S(2)}) copy-start(bf16[512,256]{1,0:T(8,128)(2,1)} %copy-done.11) | copy-start | bytes 786436
  51.8 25.2 %collective-permute-start.5 = (bf16[2,512,512]{2,1,0:T(8,128)(2,1)S(1)}, bf16[2,512,512]{2,1,0:T(8,128)(2,1)S(1)}, u32[]{:S(2)}, u32[]{:S(2)}) collective-permute-start(bf16[2,512,512]{2,1,0:T(8,128)(2,1)S(1)} %pad_maximum_fusion.refs_0_), channel_id=1, source_target_pairs={{0,16},{16,32},{32,48},{48,0},{1,17},{17,33},{33,49},{49,1},{2,18}... | collective-permute-start | bytes 3145736 | tf_op jit(solution)/shard_map/ppermute | solution.py:274
  54.8 23.6 %collective-permute-start.6 = (bf16[2,512,512]{2,1,0:T(8,128)(2,1)S(1)}, bf16[2,512,512]{2,1,0:T(8,128)(2,1)S(1)}, u32[]{:S(2)}, u32[]{:S(2)}) collective-permute-start(bf16[2,512,512]{2,1,0:T(8,128)(2,1)S(1)} %pad_maximum_fusion.refs_0_), channel_id=1, source_target_pairs={{0,48},{16,0},{32,16},{48,32},{1,49},{17,1},{33,17},{49,33},{2,50}... | collective-permute-start | bytes 3145736 | tf_op jit(solution)/shard_map/ppermute | solution.py:274
  56.0 25.1 %collective-permute-start.7 = (bf16[4,512,256]{2,1,0:T(8,128)(2,1)S(1)}, bf16[4,512,256]{2,1,0:T(8,128)(2,1)S(1)}, u32[]{:S(2)}, u32[]{:S(2)}) collective-permute-start(bf16[4,512,256]{2,1,0:T(8,128)(2,1)S(1)} %pad_maximum_fusion.1), channel_id=1, source_target_pairs={{0,64},{64,68},{4,0},{68,4},{1,65},{65,69},{5,1},{69,5},{2,66},{66... | collective-permute-start | bytes 3145736 | tf_op jit(solution)/shard_map/ppermute | solution.py:284
  57.4 23.7 %collective-permute-start.8 = (bf16[4,512,256]{2,1,0:T(8,128)(2,1)S(1)}, bf16[4,512,256]{2,1,0:T(8,128)(2,1)S(1)}, u32[]{:S(2)}, u32[]{:S(2)}) collective-permute-start(bf16[4,512,256]{2,1,0:T(8,128)(2,1)S(1)} %pad_maximum_fusion.1), channel_id=1, source_target_pairs={{0,0},{64,4},{4,64},{68,68},{1,1},{65,5},{5,65},{69,69},{2,2},{66,... | collective-permute-start | bytes 3145736 | tf_op jit(solution)/shard_map/ppermute | solution.py:284
  59.7 25.2 %copy-start.17 = (bf16[512,512]{1,0:T(8,128)(2,1)S(1)}, bf16[512,512]{1,0:T(8,128)(2,1)}, u32[]{:S(2)}) copy-start(bf16[512,512]{1,0:T(8,128)(2,1)} %param.14) | copy-start | bytes 1572868
  78.4 4.9 %copy-start.1 = (bf16[2,512,512]{2,1,0:T(8,128)(2,1)}, bf16[2,512,512]{2,1,0:T(8,128)(2,1)S(1)}, u32[]{:S(2)}) copy-start(bf16[2,512,512]{2,1,0:T(8,128)(2,1)S(1)} %collective-permute-done.6.refs_2_) | copy-start | bytes 3145732
  81.1 2.3 %copy-start.4 = (bf16[4,512,256]{2,1,0:T(8,128)(2,1)}, bf16[4,512,256]{2,1,0:T(8,128)(2,1)S(1)}, u32[]{:S(2)}) copy-start(bf16[4,512,256]{2,1,0:T(8,128)(2,1)S(1)} %collective-permute-done.7.kv_first) | copy-start | bytes 3145732
  81.1 1.0 copy-start.6
  82.1 12.7 %collective-permute-start.9 = (bf16[512,512]{1,0:T(8,128)(2,1)S(1)}, bf16[512,512]{1,0:T(8,128)(2,1)S(1)}, u32[]{:S(2)}, u32[]{:S(2)}) collective-permute-start(bf16[512,512]{1,0:T(8,128)(2,1)S(1)} %slice_bitcast_fusion.1), channel_id=1, source_target_pairs={{0,16},{16,32},{32,48},{48,0},{1,17},{17,33},{33,49},{49,1},{2,18}... | collective-permute-start | bytes 1572872 | tf_op jit(solution)/shard_map/ppermute | solution.py:274
  83.4 11.4 %collective-permute-start.10 = (bf16[512,512]{1,0:T(8,128)(2,1)S(1)}, bf16[512,512]{1,0:T(8,128)(2,1)S(1)}, u32[]{:S(2)}, u32[]{:S(2)}) collective-permute-start(bf16[512,512]{1,0:T(8,128)(2,1)S(1)} %slice_bitcast_fusion), channel_id=1, source_target_pairs={{0,48},{16,0},{32,16},{48,32},{1,49},{17,1},{33,17},{49,33},{2,50}... | collective-permute-start | bytes 1572872 | tf_op jit(solution)/shard_map/ppermute | solution.py:274
  85.0 13.9 %collective-permute-start.20 = (bf16[512,512]{1,0:T(8,128)(2,1)S(1)}, bf16[512,512]{1,0:T(8,128)(2,1)S(1)}, u32[]{:S(2)}, u32[]{:S(2)}) collective-permute-start(bf16[512,512]{1,0:T(8,128)(2,1)S(1)} %copy-done.17), channel_id=1, source_target_pairs={{0,64},{64,68},{4,0},{68,4},{1,65},{65,69},{5,1},{69,5},{2,66},{66... | collective-permute-start | bytes 1572872 | tf_op jit(solution)/shard_map/ppermute | solution.py:284
  88.4 10.5 %collective-permute-start.21 = (bf16[512,512]{1,0:T(8,128)(2,1)S(1)}, bf16[512,512]{1,0:T(8,128)(2,1)S(1)}, u32[]{:S(2)}, u32[]{:S(2)}) collective-permute-start(bf16[512,512]{1,0:T(8,128)(2,1)S(1)} %copy-done.17), channel_id=1, source_target_pairs={{0,0},{64,4},{4,64},{68,68},{1,1},{65,5},{5,65},{69,69},{2,2},{66,... | collective-permute-start | bytes 1572872 | tf_op jit(solution)/shard_map/ppermute | solution.py:284
  94.8 0.8 copy-start.8
  100.8 1.2 copy-start.2
  102.0 2.2 %copy-start.3 = (bf16[4096,512]{1,0:T(8,128)(2,1)S(1)}, bf16[4096,512]{1,0:T(8,128)(2,1)}, u32[]{:S(2)}) copy-start(bf16[4096,512]{1,0:T(8,128)(2,1)} %all-gather.5.cloned.1.call-done) | copy-start | bytes 12582916
  102.0 2.5 %copy-start.5 = (bf16[4,512,256]{2,1,0:T(8,128)(2,1)S(1)}, bf16[4,512,256]{2,1,0:T(8,128)(2,1)}, u32[]{:S(2)}) copy-start(bf16[4,512,256]{2,1,0:T(8,128)(2,1)} %copy-done.4) | copy-start | bytes 3145732
  102.0 2.8 %copy-start.7 = (bf16[4,512,256]{2,1,0:T(8,128)(2,1)S(1)}, bf16[4,512,256]{2,1,0:T(8,128)(2,1)}, u32[]{:S(2)}) copy-start(bf16[4,512,256]{2,1,0:T(8,128)(2,1)} %copy-done.6) | copy-start | bytes 3145732
  104.8 1.0 copy-start.9
  113.7 10.5 %collective-permute-start.11 = (bf16[2,256,768]{2,1,0:T(8,128)(2,1)S(1)}, bf16[2,256,768]{2,1,0:T(8,128)(2,1)S(1)}, u32[]{:S(2)}, u32[]{:S(2)}) collective-permute-start(bf16[2,256,768]{2,1,0:T(8,128)(2,1)S(1)} %get-tuple-element.49), channel_id=1, source_target_pairs={{0,8},{8,0},{1,9},{9,1},{2,10},{10,2},{3,11},{11,3},{4,12},{12,4},... | collective-permute-start | bytes 2359304 | tf_op jit(solution)/shard_map/ppermute | solution.py:274
  116.1 8.8 %collective-permute-start.17 = (bf16[2,256,768]{2,1,0:T(8,128)(2,1)S(1)}, bf16[2,256,768]{2,1,0:T(8,128)(2,1)S(1)}, u32[]{:S(2)}, u32[]{:S(2)}) collective-permute-start(bf16[2,256,768]{2,1,0:T(8,128)(2,1)S(1)} %get-tuple-element.53), channel_id=1, source_target_pairs={{0,8},{8,0},{1,9},{9,1},{2,10},{10,2},{3,11},{11,3},{4,12},{12,4},... | collective-permute-start | bytes 2359304 | tf_op jit(solution)/shard_map/ppermute | solution.py:274
  116.4 5.0 %collective-permute-start.15 = (f32[4,128]{1,0:T(4,128)S(1)}, f32[4,128]{1,0:T(4,128)S(1)}, u32[]{:S(2)}, u32[]{:S(2)}) collective-permute-start(f32[4,128]{1,0:T(4,128)S(1)} %bitcast.80), channel_id=1, source_target_pairs={{0,12},{4,8},{8,4},{12,0},{1,13},{5,9},{9,5},{13,1},{2,14},{6,10},... | collective-permute-start | bytes 6152 | tf_op jit(solution)/shard_map/ppermute | solution.py:378
  120.2 4.0 %collective-permute-start.14 = (f32[4,128]{1,0:T(4,128)S(1)}, f32[4,128]{1,0:T(4,128)S(1)}, u32[]{:S(2)}, u32[]{:S(2)}) collective-permute-start(f32[4,128]{1,0:T(4,128)S(1)} %bitcast.78), channel_id=1, source_target_pairs={{0,4},{4,0},{1,5},{5,1},{2,6},{6,2},{3,7},{7,3},{8,12},{12,8},{9,1... | collective-permute-start | bytes 6152 | tf_op jit(solution)/shard_map/ppermute | solution.py:274
  120.2 4.0 %collective-permute-start.13 = (f32[4,128]{1,0:T(4,128)S(1)}, f32[4,128]{1,0:T(4,128)S(1)}, u32[]{:S(2)}, u32[]{:S(2)}) collective-permute-start(f32[4,128]{1,0:T(4,128)S(1)} %bitcast.81), channel_id=1, source_target_pairs={{0,8},{8,0},{1,9},{9,1},{2,10},{10,2},{3,11},{11,3},{4,12},{12,4},... | collective-permute-start | bytes 6152 | tf_op jit(solution)/shard_map/ppermute | solution.py:274
  124.3 11.0 %collective-permute-start.12 = (bf16[256,768]{1,0:T(8,128)(2,1)S(1)}, bf16[256,768]{1,0:T(8,128)(2,1)S(1)}, u32[]{:S(2)}, u32[]{:S(2)}) collective-permute-start(bf16[256,768]{1,0:T(8,128)(2,1)S(1)} %fusion), channel_id=1, source_target_pairs={{0,4},{4,0},{1,5},{5,1},{2,6},{6,2},{3,7},{7,3},{8,12},{12,8},{9,1... | collective-permute-start | bytes 1179656 | tf_op jit(solution)/shard_map/ppermute | solution.py:274
  125.1 18.7 %collective-permute-start.18 = (bf16[256,768]{1,0:T(8,128)(2,1)S(1)}, bf16[256,768]{1,0:T(8,128)(2,1)S(1)}, u32[]{:S(2)}, u32[]{:S(2)}) collective-permute-start(bf16[256,768]{1,0:T(8,128)(2,1)S(1)} %fusion.1), channel_id=1, source_target_pairs={{0,4},{4,0},{1,5},{5,1},{2,6},{6,2},{3,7},{7,3},{8,12},{12,8},{9,1... | collective-permute-start | bytes 1179656 | tf_op jit(solution)/shard_map/ppermute | solution.py:274
  136.4 13.0 %collective-permute-start.16 = (bf16[256,512]{1,0:T(8,128)(2,1)S(1)}, bf16[256,512]{1,0:T(8,128)(2,1)S(1)}, u32[]{:S(2)}, u32[]{:S(2)}) collective-permute-start(bf16[256,512]{1,0:T(8,128)(2,1)S(1)} %attend.2.refs_0_), channel_id=1, source_target_pairs={{0,4},{4,0},{1,5},{5,1},{2,6},{6,2},{3,7},{7,3},{8,12},{12,8},{9,1... | collective-permute-start | bytes 786440 | tf_op jit(solution)/shard_map/ppermute | solution.py:274
  144.8 9.5 %collective-permute-start.19 = (bf16[256,512]{1,0:T(8,128)(2,1)S(1)}, bf16[256,512]{1,0:T(8,128)(2,1)S(1)}, u32[]{:S(2)}, u32[]{:S(2)}) collective-permute-start(bf16[256,512]{1,0:T(8,128)(2,1)S(1)} %attend.3.refs_2_), channel_id=1, source_target_pairs={{0,4},{4,0},{1,5},{5,1},{2,6},{6,2},{3,7},{7,3},{8,12},{12,8},{9,1... | collective-permute-start | bytes 786440 | tf_op jit(solution)/shard_map/ppermute | solution.py:274
  154.3 3.4 %copy-start = (bf16[16,512,512]{2,1,0:T(8,128)(2,1)S(1)}, bf16[16,512,512]{2,1,0:T(8,128)(2,1)}, u32[]{:S(2)}) copy-start(bf16[16,512,512]{2,1,0:T(8,128)(2,1)} %all-gather.7.cloned.1.call-done) | copy-start | bytes 25165828
  159.5 12.3 %collective-permute-start.26 = (bf16[256,1024]{1,0:T(8,128)(2,1)S(1)}, bf16[256,1024]{1,0:T(8,128)(2,1)S(1)}, u32[]{:S(2)}, u32[]{:S(2)}) collective-permute-start(bf16[256,1024]{1,0:T(8,128)(2,1)S(1)} %get-tuple-element.61), channel_id=1, source_target_pairs={{0,3},{1,0},{2,1},{3,2},{4,7},{5,4},{6,5},{7,6},{8,11},{9,8},{10,9... | collective-permute-start | bytes 1572872 | tf_op jit(solution)/shard_map/ppermute | solution.py:274
  163.3 12.2 %collective-permute-start.22 = (bf16[256,1024]{1,0:T(8,128)(2,1)S(1)}, bf16[256,1024]{1,0:T(8,128)(2,1)S(1)}, u32[]{:S(2)}, u32[]{:S(2)}) collective-permute-start(bf16[256,1024]{1,0:T(8,128)(2,1)S(1)} %get-tuple-element.60), channel_id=1, source_target_pairs={{0,1},{1,2},{2,3},{3,0},{4,5},{5,6},{6,7},{7,4},{8,9},{9,10},{10,1... | collective-permute-start | bytes 1572872 | tf_op jit(solution)/shard_map/ppermute | solution.py:274
  167.3 18.8 %collective-permute-start.25 = (bf16[256,1024]{1,0:T(8,128)(2,1)S(1)}, bf16[256,1024]{1,0:T(8,128)(2,1)S(1)}, u32[]{:S(2)}, u32[]{:S(2)}) collective-permute-start(bf16[256,1024]{1,0:T(8,128)(2,1)S(1)} %get-tuple-element.67), channel_id=1, source_target_pairs={{0,1},{1,2},{2,3},{3,0},{4,5},{5,6},{6,7},{7,4},{8,9},{9,10},{10,1... | collective-permute-start | bytes 1572872 | tf_op jit(solution)/shard_map/ppermute | solution.py:274
  171.9 14.2 %collective-permute-start.27 = (bf16[256,1024]{1,0:T(8,128)(2,1)S(1)}, bf16[256,1024]{1,0:T(8,128)(2,1)S(1)}, u32[]{:S(2)}, u32[]{:S(2)}) collective-permute-start(bf16[256,1024]{1,0:T(8,128)(2,1)S(1)} %add_convert_fusion.1), channel_id=1, source_target_pairs={{0,3},{1,0},{2,1},{3,2},{4,7},{5,4},{6,5},{7,6},{8,11},{9,8},{10,9... | collective-permute-start | bytes 1572872 | tf_op jit(solution)/shard_map/ppermute | solution.py:274
  175.4 18.8 %collective-permute-start.24 = (bf16[256,1024]{1,0:T(8,128)(2,1)S(1)}, bf16[256,1024]{1,0:T(8,128)(2,1)S(1)}, u32[]{:S(2)}, u32[]{:S(2)}) collective-permute-start(bf16[256,1024]{1,0:T(8,128)(2,1)S(1)} %get-tuple-element.65), channel_id=1, source_target_pairs={{0,3},{1,0},{2,1},{3,2},{4,7},{5,4},{6,5},{7,6},{8,11},{9,8},{10,9... | collective-permute-start | bytes 1572872 | tf_op jit(solution)/shard_map/ppermute | solution.py:274
  175.7 21.6 %collective-permute-start.23 = (bf16[256,1024]{1,0:T(8,128)(2,1)S(1)}, bf16[256,1024]{1,0:T(8,128)(2,1)S(1)}, u32[]{:S(2)}, u32[]{:S(2)}) collective-permute-start(bf16[256,1024]{1,0:T(8,128)(2,1)S(1)} %add_convert_fusion.3), channel_id=1, source_target_pairs={{0,1},{1,2},{2,3},{3,0},{4,5},{5,6},{6,7},{7,4},{8,9},{9,10},{10,1... | collective-permute-start | bytes 1572872 | tf_op jit(solution)/shard_map/ppermute | solution.py:274
Sparse Core Ops, SparseCore 0:
  50.6 50.0 all-gather.4
  102.4 50.6 all-gather.6
where the time goes:
time: 209 us; the launch traced here: 206 us
  waiting for transfers between devices  103 us (49%)
  starting transfers between devices  48 us (23%)
  Pallas kernels  20.8 us (10%)
  between operations  13.8 us (7%)
  local copies, waits for them, and re-layouts  11.7 us (6%)
  other arithmetic  8.71 us (4%)
    ppermute x21, waiting for transfers between devices, shift(): return lax.ppermute(x, axis, [(i, (i + by) % size) for i in range(size)])  95.1 us
    ppermute x21, starting transfers between devices, shift(): return lax.ppermute(x, axis, [(i, (i + by) % size) for i in range(size)])  27.9 us
    unnamed x36, local copies, waits for them, and re-layouts  10 us
    ppermute x6, starting transfers between devices, spread(): lax.ppermute(x, ('xl', 'xh'), [(at(a), at(b)) for a, b in pairs])  9.28 us
    pallas_call x1, Pallas kernels, project(): pl.pallas_call(project_kernel, in_specs=[SMEM] + [VMEM] * 6, out_specs=[V...  7.86 us
    all_to_all x1, starting transfers between devices, local(): lax.all_to_all(outgoing, dp, split_axis=0, concat_axis=0, tiled=True)  7.05 us
    ppermute x6, waiting for transfers between devices, spread(): lax.ppermute(x, ('xl', 'xh'), [(at(a), at(b)) for a, b in pairs])  5.91 us
    pallas_call x2, Pallas kernels, expand(): pl.pallas_call(functools.partial(expand_kernel, steps), in_specs=[SMEM] +...  5.77 us
  transfers between devices with their start and end apart: 31, of which 18 were waited for; matrix products, arithmetic and copies ran while one was open for 4% of the time, Pallas kernels for 7%

commit v1 on v0

--- a/solution.py
+++ b/solution.py
@@ -382,7 +382,7 @@
     nears = [shift(send, "c", 1) for send in sends]
     others = [(keep[1] + near[1].astype(F32)).astype(BF) for keep, near in zip(keeps, nears)]
     across_low = shift(others[0], "xh", 1)
-    across_high = shift(after((others[1],), squares)[0], "xh", 1)
+    across_high = shift(after((others[1],), squares, across_low)[0], "xh", 1)
     acrosses = [across_low, across_high]
     mean = squares * (1.0 / norm_gain.shape[0])
     attns = [

time: 209 us -> 208 us (level)
  waiting for transfers between devices: 103 us -> 100 us
  starting transfers between devices: 48 us -> 50.2 us
    ppermute x21, starting transfers between devices: 27.9 us -> 30.1 us  [shift(): return lax.ppermute(x, axis, [(i, (i + by) % size) for i in range(size)])]
  transfers between devices with their start and end apart: 31 -> 31, of which waited for: 18 -> 17; matrix products, arithmetic and copies ran while one was open for 4% -> 4% of each run, Pallas kernels for 7% -> 7%
where the time goes in v1:
time: 208 us; the launch traced here: 205 us
  waiting for transfers between devices  100 us (48%)
  starting transfers between devices  50.2 us (24%)
  Pallas kernels  20.8 us (10%)
  between operations  13.8 us (7%)
  local copies, waits for them, and re-layouts  11.7 us (6%)
  other arithmetic  8.71 us (4%)
    ppermute x21, waiting for transfers between devices, shift(): return lax.ppermute(x, axis, [(i, (i + by) % size) for i in range(size)])  93.4 us
    ppermute x21, starting transfers between devices, shift(): return lax.ppermute(x, axis, [(i, (i + by) % size) for i in range(size)])  30.1 us
    unnamed x36, local copies, waits for them, and re-layouts  10 us
    ppermute x6, starting transfers between devices, spread(): lax.ppermute(x, ('xl', 'xh'), [(at(a), at(b)) for a, b in pairs])  9.28 us
    pallas_call x1, Pallas kernels, project(): pl.pallas_call(project_kernel, in_specs=[SMEM] + [VMEM] * 6, out_specs=[V...  7.86 us
    all_to_all x1, starting transfers between devices, local(): lax.all_to_all(outgoing, dp, split_axis=0, concat_axis=0, tiled=True)  7.05 us
    ppermute x6, waiting for transfers between devices, spread(): lax.ppermute(x, ('xl', 'xh'), [(at(a), at(b)) for a, b in pairs])  5.91 us
    pallas_call x2, Pallas kernels, expand(): pl.pallas_call(functools.partial(expand_kernel, steps), in_specs=[SMEM] +...  5.77 us
  transfers between devices with their start and end apart: 31, of which 17 were waited for; matrix products, arithmetic and copies ran while one was open for 4% of the time, Pallas kernels for 7%

profile of v1, /device:TPU:1, one launch (start us, length us, event | category | flops | bytes accessed | tf_op | source)
XLA Modules:
  0.0 205.2 jit_solution(7971160140135131047)
XLA Ops:
  6.5 2.8 %dispatch.1 = bf16[8,2,2,48,512]{4,3,2,1,0:T(8,128)(2,1)} custom-call(s32[1]{0:T(128)} %bitcast.12.place, s32[256]{0:T(256)} %pair_row.1, bf16[16,48,1024]{2,1,0:T(8,128)(2,1)} %pairs.1), custom_call_target="tpu_custom_call" | custom-call | bytes 3145728 | tf_op jit(solution)/shard_map/dispatch/pallas_call | solution.py:44
  9.3 7.0 %all-to-all-start = ((bf16[16,2,48,512]{3,2,1,0:T(8,128)(2,1)}), bf16[16,2,48,512]{3,2,1,0:T(8,128)(2,1)S(1)}, u32[]{:S(2)}, u32[]{:S(2)}) async-start(bf16[16,2,48,512]{3,2,1,0:T(8,128)(2,1)} %bitcast.72), calls=%async_computation | async-start | bytes 3145728 | tf_op jit(solution)/shard_map/all_to_all | solution.py:330
  16.5 0.8 dynamic_slice.3
  17.4 1.5 collective-permute-start
  18.9 1.4 collective-permute-start.1
  20.3 1.0 multiply_convert_fusion.1
  21.3 1.3 collective-permute-start.2
  22.6 1.5 collective-permute-start.3
  24.1 1.5 collective-permute-start.4
  26.5 16.1 %collective-permute-done.2 = bf16[512,256]{1,0:T(8,128)(2,1)S(1)} collective-permute-done((bf16[512,256]{1,0:T(8,128)(2,1)S(1)}, bf16[512,256]{1,0:T(8,128)(2,1)S(1)}, u32[]{:S(2)}, u32[]{:S(2)}) %collective-permute-start.2) | collective-permute-done | bytes 262176 | tf_op jit(solution)/shard_map/ppermute | solution.py:274
  42.6 5.9 %collective-permute-done.4 = bf16[512,256]{1,0:T(8,128)(2,1)} collective-permute-done((bf16[512,256]{1,0:T(8,128)(2,1)S(1)}, bf16[512,256]{1,0:T(8,128)(2,1)}, u32[]{:S(2)}, u32[]{:S(2)}) %collective-permute-start.4) | collective-permute-done | bytes 262176 | tf_op jit(solution)/shard_map/ppermute | solution.py:274
  48.5 2.0 pack.1
  50.6 1.1 pad_maximum_fusion.refs_0_
  51.8 3.1 %collective-permute-start.5 = (bf16[2,512,512]{2,1,0:T(8,128)(2,1)S(1)}, bf16[2,512,512]{2,1,0:T(8,128)(2,1)S(1)}, u32[]{:S(2)}, u32[]{:S(2)}) collective-permute-start(bf16[2,512,512]{2,1,0:T(8,128)(2,1)S(1)} %pad_maximum_fusion.refs_0_), channel_id=1, source_target_pairs={{0,16},{16,32},{32,48},{48,0},{1,17},{17,33},{33,49},{49,1},{2,18}... | collective-permute-start | bytes 3145736 | tf_op jit(solution)/shard_map/ppermute | solution.py:274
  54.8 1.2 pad_maximum_fusion.1
  56.0 1.4 collective-permute-start.7
  57.4 0.7 collective-permute-start.8
  58.1 0.3 convert_reduce_fusion
  58.5 1.0 multiply_cosine_fusion
  59.4 0.3 pad_maximum_fusion.4
  59.8 17.2 %collective-permute-done.5.refs_1_ = bf16[2,512,512]{2,1,0:T(8,128)(2,1)S(1)} collective-permute-done((bf16[2,512,512]{2,1,0:T(8,128)(2,1)S(1)}, bf16[2,512,512]{2,1,0:T(8,128)(2,1)S(1)}, u32[]{:S(2)}, u32[]{:S(2)}) %collective-permute-start.5) | collective-permute-done | bytes 1048608 | tf_op jit(solution)/shard_map/ppermute | solution.py:274
  77.0 1.5 collective-permute-done.6.refs_2_
  78.4 2.6 %collective-permute-done.7.kv_first = bf16[4,512,256]{2,1,0:T(8,128)(2,1)S(1)} collective-permute-done((bf16[4,512,256]{2,1,0:T(8,128)(2,1)S(1)}, bf16[4,512,256]{2,1,0:T(8,128)(2,1)S(1)}, u32[]{:S(2)}, u32[]{:S(2)}) %collective-permute-start.7) | collective-permute-done | bytes 1048608 | tf_op jit(solution)/shard_map/ppermute | solution.py:284
  81.1 1.0 copy-done.6
  82.1 1.3 collective-permute-start.9
  83.4 1.6 collective-permute-start.10
  85.0 3.4 %collective-permute-start.20 = (bf16[512,512]{1,0:T(8,128)(2,1)S(1)}, bf16[512,512]{1,0:T(8,128)(2,1)S(1)}, u32[]{:S(2)}, u32[]{:S(2)}) collective-permute-start(bf16[512,512]{1,0:T(8,128)(2,1)S(1)} %copy-done.17), channel_id=1, source_target_pairs={{0,64},{64,68},{4,0},{68,4},{1,65},{65,69},{5,1},{69,5},{2,66},{66... | collective-permute-start | bytes 1572872 | tf_op jit(solution)/shard_map/ppermute | solution.py:284
  88.4 0.9 collective-permute-start.21
  89.3 5.5 %collective-permute-done.9.far_low = bf16[512,512]{1,0:T(8,128)(2,1)S(1)} collective-permute-done((bf16[512,512]{1,0:T(8,128)(2,1)S(1)}, bf16[512,512]{1,0:T(8,128)(2,1)S(1)}, u32[]{:S(2)}, u32[]{:S(2)}) %collective-permute-start.9) | collective-permute-done | bytes 524320 | tf_op jit(solution)/shard_map/ppermute | solution.py:274
  94.8 0.8 copy-done.8
  95.6 3.3 %collective-permute-done.20 = bf16[512,512]{1,0:T(8,128)(2,1)S(1)} collective-permute-done((bf16[512,512]{1,0:T(8,128)(2,1)S(1)}, bf16[512,512]{1,0:T(8,128)(2,1)S(1)}, u32[]{:S(2)}, u32[]{:S(2)}) %collective-permute-start.20) | collective-permute-done | bytes 524320 | tf_op jit(solution)/shard_map/ppermute | solution.py:284
  98.9 1.1 pad_maximum_fusion.2
  100.0 0.6 all-gather.5.cloned.1.call-done
  100.8 1.2 copy-done.2
  102.2 1.9 copy-done.3
  104.2 0.3 copy-done.5
  104.5 0.3 copy-done.7
  104.8 1.0 copy-done.9
  105.8 7.9 %project.1 = (f32[2,256,768]{2,1,0:T(8,128)S(1)}, f32[2,256,768]{2,1,0:T(8,128)S(1)}, bf16[2,256,768]{2,1,0:T(8,128)(2,1)S(1)}, bf16[2,256,768]{2,1,0:T(8,128)(2,1)S(1)}, f32[2,512,1]{2,1,0:T(8,128)S(1)}) custom-call(s32[4]{0:T(128)S(1)} %pad_add_fusion.place, bf16[4,1024,512]{2,1,0:T(8,128)(2,1)S(1)} %bitcast.71, bf16[3,2,512,512]{3,2,1,0:T(8,128)(2,1)S(1)} %stage.1.w_q, ...), custom_call_target="tpu_custom_call" | custom-call | flops 6442450944 | bytes 10485760 | tf_op jit(solution)/shard_map/project/pallas_call | solution.py:148
  113.7 2.4 %collective-permute-start.11 = (bf16[2,256,768]{2,1,0:T(8,128)(2,1)S(1)}, bf16[2,256,768]{2,1,0:T(8,128)(2,1)S(1)}, u32[]{:S(2)}, u32[]{:S(2)}) collective-permute-start(bf16[2,256,768]{2,1,0:T(8,128)(2,1)S(1)} %get-tuple-element.49), channel_id=1, source_target_pairs={{0,8},{8,0},{1,9},{9,1},{2,10},{10,2},{3,11},{11,3},{4,12},{12,4},... | collective-permute-start | bytes 2359304 | tf_op jit(solution)/shard_map/ppermute | solution.py:274
  116.4 3.7 %collective-permute-start.15 = (f32[4,128]{1,0:T(4,128)S(1)}, f32[4,128]{1,0:T(4,128)S(1)}, u32[]{:S(2)}, u32[]{:S(2)}) collective-permute-start(f32[4,128]{1,0:T(4,128)S(1)} %bitcast.80), channel_id=1, source_target_pairs={{0,12},{4,8},{8,4},{12,0},{1,13},{5,9},{9,5},{13,1},{2,14},{6,10},... | collective-permute-start | bytes 6152 | tf_op jit(solution)/shard_map/ppermute | solution.py:378
  120.5 2.9 %collective-permute-start.12 = (bf16[256,768]{1,0:T(8,128)(2,1)S(1)}, bf16[256,768]{1,0:T(8,128)(2,1)S(1)}, u32[]{:S(2)}, u32[]{:S(2)}) collective-permute-start(bf16[256,768]{1,0:T(8,128)(2,1)S(1)} %fusion), channel_id=1, source_target_pairs={{0,4},{4,0},{1,5},{5,1},{2,6},{6,2},{3,7},{7,3},{8,12},{12,8},{9,1... | collective-permute-start | bytes 1179656 | tf_op jit(solution)/shard_map/ppermute | solution.py:274
  123.4 0.9 collective-permute-done.14
  124.4 8.1 %collective-permute-done.12.across = bf16[256,768]{1,0:T(8,128)(2,1)S(1)} collective-permute-done((bf16[256,768]{1,0:T(8,128)(2,1)S(1)}, bf16[256,768]{1,0:T(8,128)(2,1)S(1)}, u32[]{:S(2)}, u32[]{:S(2)}) %collective-permute-start.12) | collective-permute-done | bytes 393248 | tf_op jit(solution)/shard_map/ppermute | solution.py:274
  132.4 2.5 %collective-permute-start.18 = (bf16[256,768]{1,0:T(8,128)(2,1)S(1)}, bf16[256,768]{1,0:T(8,128)(2,1)S(1)}, u32[]{:S(2)}, u32[]{:S(2)}) collective-permute-start(bf16[256,768]{1,0:T(8,128)(2,1)S(1)} %fusion.1), channel_id=1, source_target_pairs={{0,4},{4,0},{1,5},{5,1},{2,6},{6,2},{3,7},{7,3},{8,12},{12,8},{9,1... | collective-permute-start | bytes 1179656 | tf_op jit(solution)/shard_map/ppermute | solution.py:274
  134.9 1.1 attend.2.refs_0_
  136.0 0.6 collective-permute-start.16
  136.6 6.8 %collective-permute-done.18.across = bf16[256,768]{1,0:T(8,128)(2,1)S(1)} collective-permute-done((bf16[256,768]{1,0:T(8,128)(2,1)S(1)}, bf16[256,768]{1,0:T(8,128)(2,1)S(1)}, u32[]{:S(2)}, u32[]{:S(2)}) %collective-permute-start.18) | collective-permute-done | bytes 393248 | tf_op jit(solution)/shard_map/ppermute | solution.py:274
  143.4 1.1 attend.3.refs_2_
  144.5 2.4 %collective-permute-start.19 = (bf16[256,512]{1,0:T(8,128)(2,1)S(1)}, bf16[256,512]{1,0:T(8,128)(2,1)S(1)}, u32[]{:S(2)}, u32[]{:S(2)}) collective-permute-start(bf16[256,512]{1,0:T(8,128)(2,1)S(1)} %attend.3.refs_2_), channel_id=1, source_target_pairs={{0,4},{4,0},{1,5},{5,1},{2,6},{6,2},{3,7},{7,3},{8,12},{12,8},{9,1... | collective-permute-start | bytes 786440 | tf_op jit(solution)/shard_map/ppermute | solution.py:274
  146.8 2.2 %collective-permute-done.16.refs_1_ = bf16[256,512]{1,0:T(8,128)(2,1)S(1)} collective-permute-done((bf16[256,512]{1,0:T(8,128)(2,1)S(1)}, bf16[256,512]{1,0:T(8,128)(2,1)S(1)}, u32[]{:S(2)}, u32[]{:S(2)}) %collective-permute-start.16) | collective-permute-done | bytes 262176 | tf_op jit(solution)/shard_map/ppermute | solution.py:274
  149.0 5.0 %collective-permute-done.19.refs_3_ = bf16[256,512]{1,0:T(8,128)(2,1)S(1)} collective-permute-done((bf16[256,512]{1,0:T(8,128)(2,1)S(1)}, bf16[256,512]{1,0:T(8,128)(2,1)S(1)}, u32[]{:S(2)}, u32[]{:S(2)}) %collective-permute-start.19) | collective-permute-done | bytes 262176 | tf_op jit(solution)/shard_map/ppermute | solution.py:274
  154.0 3.4 %copy-done = bf16[16,512,512]{2,1,0:T(8,128)(2,1)S(1)} copy-done((bf16[16,512,512]{2,1,0:T(8,128)(2,1)S(1)}, bf16[16,512,512]{2,1,0:T(8,128)(2,1)}, u32[]{:S(2)}) %copy-start) | copy-done | bytes 8388632
  157.3 1.8 expand.2
  159.2 3.8 %collective-permute-start.26 = (bf16[256,1024]{1,0:T(8,128)(2,1)S(1)}, bf16[256,1024]{1,0:T(8,128)(2,1)S(1)}, u32[]{:S(2)}, u32[]{:S(2)}) collective-permute-start(bf16[256,1024]{1,0:T(8,128)(2,1)S(1)} %get-tuple-element.61), channel_id=1, source_target_pairs={{0,3},{1,0},{2,1},{3,2},{4,7},{5,4},{6,5},{7,6},{8,11},{9,8},{10,9... | collective-permute-start | bytes 1572872 | tf_op jit(solution)/shard_map/ppermute | solution.py:274
  163.0 4.0 %expand.3 = (bf16[256,1024]{1,0:T(8,128)(2,1)S(1)}, bf16[256,1024]{1,0:T(8,128)(2,1)S(1)}, bf16[256,1024]{1,0:T(8,128)(2,1)S(1)}, bf16[256,1024]{1,0:T(8,128)(2,...) custom-call(s32[4]{0:T(128)S(1)} %pad_add_fusion.place, bf16[256,512]{1,0:T(8,128)(2,1)S(1)} %attend.2.refs_0_, ...), custom_call_target="tpu_custom_call" | custom-call | flops 3221225472 | bytes 18874368 | tf_op jit(solution)/shard_map/expand/pallas_call | solution.py:257
  167.0 4.4 %collective-permute-done.26 = bf16[256,1024]{1,0:T(8,128)(2,1)S(1)} collective-permute-done((bf16[256,1024]{1,0:T(8,128)(2,1)S(1)}, bf16[256,1024]{1,0:T(8,128)(2,1)S(1)}, u32[]{:S(2)}, u32[]{:S(2)}) %collective-permute-start.26) | collective-permute-done | bytes 524320 | tf_op jit(solution)/shard_map/ppermute | solution.py:274
  171.6 3.5 %collective-permute-start.27 = (bf16[256,1024]{1,0:T(8,128)(2,1)S(1)}, bf16[256,1024]{1,0:T(8,128)(2,1)S(1)}, u32[]{:S(2)}, u32[]{:S(2)}) collective-permute-start(bf16[256,1024]{1,0:T(8,128)(2,1)S(1)} %add_convert_fusion.1), channel_id=1, source_target_pairs={{0,3},{1,0},{2,1},{3,2},{4,7},{5,4},{6,5},{7,6},{8,11},{9,8},{10,9... | collective-permute-start | bytes 1572872 | tf_op jit(solution)/shard_map/ppermute | solution.py:274
  175.4 1.5 collective-permute-start.23
  176.9 9.0 %collective-permute-done.25 = bf16[256,1024]{1,0:T(8,128)(2,1)S(1)} collective-permute-done((bf16[256,1024]{1,0:T(8,128)(2,1)S(1)}, bf16[256,1024]{1,0:T(8,128)(2,1)S(1)}, u32[]{:S(2)}, u32[]{:S(2)}) %collective-permute-start.25) | collective-permute-done | bytes 524320 | tf_op jit(solution)/shard_map/ppermute | solution.py:274
  185.8 0.3 add_convert_fusion
  186.1 7.8 %collective-permute-done.24 = bf16[256,1024]{1,0:T(8,128)(2,1)S(1)} collective-permute-done((bf16[256,1024]{1,0:T(8,128)(2,1)S(1)}, bf16[256,1024]{1,0:T(8,128)(2,1)S(1)}, u32[]{:S(2)}, u32[]{:S(2)}) %collective-permute-start.24) | collective-permute-done | bytes 524320 | tf_op jit(solution)/shard_map/ppermute | solution.py:274
  193.9 3.1 %collective-permute-done.23 = bf16[256,1024]{1,0:T(8,128)(2,1)S(1)} collective-permute-done((bf16[256,1024]{1,0:T(8,128)(2,1)S(1)}, bf16[256,1024]{1,0:T(8,128)(2,1)S(1)}, u32[]{:S(2)}, u32[]{:S(2)}) %collective-permute-start.23) | collective-permute-done | bytes 524320 | tf_op jit(solution)/shard_map/ppermute | solution.py:274
  197.3 1.0 pad_maximum_fusion.3
  (87 shorter events, 3.3 us)
Async XLA Ops:
  9.3 7.9 %copy-start.10 = (bf16[512,512]{1,0:T(8,128)(2,1)S(1)}, bf16[512,512]{1,0:T(8,128)(2,1)}, u32[]{:S(2)}) copy-start(bf16[512,512]{1,0:T(8,128)(2,1)} %param.11) | copy-start | bytes 1572868
  9.3 11.0 %copy-start.13 = (bf16[512,128]{1,0:T(8,128)(2,1)S(1)}, bf16[512,128]{1,0:T(8,128)(2,1)}, u32[]{:S(2)}) copy-start(bf16[512,128]{1,0:T(8,128)(2,1)} %param.13) | copy-start | bytes 393220
  9.3 39.2 %all-to-all-start = ((bf16[16,2,48,512]{3,2,1,0:T(8,128)(2,1)}), bf16[16,2,48,512]{3,2,1,0:T(8,128)(2,1)S(1)}, u32[]{:S(2)}, u32[]{:S(2)}) async-start(bf16[16,2,48,512]{3,2,1,0:T(8,128)(2,1)} %bitcast.72), calls=%async_computation | async-start | bytes 3145728 | tf_op jit(solution)/shard_map/all_to_all | solution.py:330
  16.4 9.2 %copy-start.16 = (s32[256,2]{0,1:T(2,128)S(1)}, s32[256,2]{0,1:T(2,128)}, u32[]{:S(2)}) copy-start(s32[256,2]{0,1:T(2,128)} %param.16) | copy-start | bytes 6148
  16.4 9.2 %copy-start.15 = (s32[256]{0:T(256)S(1)}, s32[256]{0:T(256)}, u32[]{:S(2)}) copy-start(s32[256]{0:T(256)} %pair_row.1) | copy-start | bytes 3076
  16.4 84.2 %all-gather.5.cloned.1.call-start = ((), (), s32[]{:S(2)}) async-start(), calls=%async_computation.1 | async-start | bytes 5242880 | tf_op jit(solution)/shard_map/all_gather | solution.py:347
  17.4 31.1 %collective-permute-start = (bf16[512,512]{1,0:T(8,128)(2,1)S(1)}, bf16[512,512]{1,0:T(8,128)(2,1)S(1)}, u32[]{:S(2)}, u32[]{:S(2)}) collective-permute-start(bf16[512,512]{1,0:T(8,128)(2,1)S(1)} %multiply_convert_fusion), channel_id=1, source_target_pairs={{0,64},{64,68},{4,0},{68,4},{1,65},{65,69},{5,1},{69,5},{2,66},{66... | collective-permute-start | bytes 1572872 | tf_op jit(solution)/shard_map/ppermute | solution.py:284
  18.9 29.6 %collective-permute-start.1 = (bf16[512,512]{1,0:T(8,128)(2,1)S(1)}, bf16[512,512]{1,0:T(8,128)(2,1)}, u32[]{:S(2)}, u32[]{:S(2)}) collective-permute-start(bf16[512,512]{1,0:T(8,128)(2,1)S(1)} %multiply_convert_fusion), channel_id=1, source_target_pairs={{0,0},{64,4},{4,64},{68,68},{1,1},{65,5},{5,65},{69,69},{2,2},{66,... | collective-permute-start | bytes 1572872 | tf_op jit(solution)/shard_map/ppermute | solution.py:284
  21.3 21.2 %collective-permute-start.2 = (bf16[512,256]{1,0:T(8,128)(2,1)S(1)}, bf16[512,256]{1,0:T(8,128)(2,1)S(1)}, u32[]{:S(2)}, u32[]{:S(2)}) collective-permute-start(bf16[512,256]{1,0:T(8,128)(2,1)S(1)} %multiply_convert_fusion.1), channel_id=1, source_target_pairs={{0,16},{16,32},{32,48},{48,0},{1,17},{17,33},{33,49},{49,1},{2,18}... | collective-permute-start | bytes 786440 | tf_op jit(solution)/shard_map/ppermute | solution.py:274
  22.6 20.0 %collective-permute-start.3 = (bf16[512,256]{1,0:T(8,128)(2,1)S(1)}, bf16[512,256]{1,0:T(8,128)(2,1)}, u32[]{:S(2)}, u32[]{:S(2)}) collective-permute-start(bf16[512,256]{1,0:T(8,128)(2,1)S(1)} %multiply_convert_fusion.1), channel_id=1, source_target_pairs={{0,48},{16,0},{32,16},{48,32},{1,49},{17,1},{33,17},{49,33},{2,50}... | collective-permute-start | bytes 786440 | tf_op jit(solution)/shard_map/ppermute | solution.py:274
  24.1 24.4 %collective-permute-start.4 = (bf16[512,256]{1,0:T(8,128)(2,1)S(1)}, bf16[512,256]{1,0:T(8,128)(2,1)}, u32[]{:S(2)}, u32[]{:S(2)}) collective-permute-start(bf16[512,256]{1,0:T(8,128)(2,1)S(1)} %multiply_convert_fusion.1), channel_id=1, source_target_pairs={{0,32},{16,48},{32,0},{48,16},{1,33},{17,49},{33,1},{49,17},{2,34}... | collective-permute-start | bytes 786440 | tf_op jit(solution)/shard_map/ppermute | solution.py:274
  26.5 24.1 %copy-start.14 = (s32[512]{0:T(512)S(1)}, s32[512]{0:T(512)}, u32[]{:S(2)}) copy-start(s32[512]{0:T(512)} %param.17) | copy-start | bytes 6148
  42.6 7.9 %copy-start.11 = (bf16[512,256]{1,0:T(8,128)(2,1)}, bf16[512,256]{1,0:T(8,128)(2,1)S(1)}, u32[]{:S(2)}) copy-start(bf16[512,256]{1,0:T(8,128)(2,1)S(1)} %collective-permute-done.2) | copy-start | bytes 786436
  50.5 103.5 %all-gather.7.cloned.1.call-start = ((), (), s32[]{:S(2)}) async-start(), calls=%async_computation.2 | async-start | bytes 9437184 | tf_op jit(solution)/shard_map/all_gather | solution.py:371
  50.5 4.3 %copy-start.12 = (bf16[512,256]{1,0:T(8,128)(2,1)S(1)}, bf16[512,256]{1,0:T(8,128)(2,1)}, u32[]{:S(2)}) copy-start(bf16[512,256]{1,0:T(8,128)(2,1)} %copy-done.11) | copy-start | bytes 786436
  51.8 25.2 %collective-permute-start.5 = (bf16[2,512,512]{2,1,0:T(8,128)(2,1)S(1)}, bf16[2,512,512]{2,1,0:T(8,128)(2,1)S(1)}, u32[]{:S(2)}, u32[]{:S(2)}) collective-permute-start(bf16[2,512,512]{2,1,0:T(8,128)(2,1)S(1)} %pad_maximum_fusion.refs_0_), channel_id=1, source_target_pairs={{0,16},{16,32},{32,48},{48,0},{1,17},{17,33},{33,49},{49,1},{2,18}... | collective-permute-start | bytes 3145736 | tf_op jit(solution)/shard_map/ppermute | solution.py:274
  54.8 23.6 %collective-permute-start.6 = (bf16[2,512,512]{2,1,0:T(8,128)(2,1)S(1)}, bf16[2,512,512]{2,1,0:T(8,128)(2,1)S(1)}, u32[]{:S(2)}, u32[]{:S(2)}) collective-permute-start(bf16[2,512,512]{2,1,0:T(8,128)(2,1)S(1)} %pad_maximum_fusion.refs_0_), channel_id=1, source_target_pairs={{0,48},{16,0},{32,16},{48,32},{1,49},{17,1},{33,17},{49,33},{2,50}... | collective-permute-start | bytes 3145736 | tf_op jit(solution)/shard_map/ppermute | solution.py:274
  56.0 25.1 %collective-permute-start.7 = (bf16[4,512,256]{2,1,0:T(8,128)(2,1)S(1)}, bf16[4,512,256]{2,1,0:T(8,128)(2,1)S(1)}, u32[]{:S(2)}, u32[]{:S(2)}) collective-permute-start(bf16[4,512,256]{2,1,0:T(8,128)(2,1)S(1)} %pad_maximum_fusion.1), channel_id=1, source_target_pairs={{0,64},{64,68},{4,0},{68,4},{1,65},{65,69},{5,1},{69,5},{2,66},{66... | collective-permute-start | bytes 3145736 | tf_op jit(solution)/shard_map/ppermute | solution.py:284
  57.4 23.7 %collective-permute-start.8 = (bf16[4,512,256]{2,1,0:T(8,128)(2,1)S(1)}, bf16[4,512,256]{2,1,0:T(8,128)(2,1)S(1)}, u32[]{:S(2)}, u32[]{:S(2)}) collective-permute-start(bf16[4,512,256]{2,1,0:T(8,128)(2,1)S(1)} %pad_maximum_fusion.1), channel_id=1, source_target_pairs={{0,0},{64,4},{4,64},{68,68},{1,1},{65,5},{5,65},{69,69},{2,2},{66,... | collective-permute-start | bytes 3145736 | tf_op jit(solution)/shard_map/ppermute | solution.py:284
  59.7 25.2 %copy-start.17 = (bf16[512,512]{1,0:T(8,128)(2,1)S(1)}, bf16[512,512]{1,0:T(8,128)(2,1)}, u32[]{:S(2)}) copy-start(bf16[512,512]{1,0:T(8,128)(2,1)} %param.14) | copy-start | bytes 1572868
  78.4 4.9 %copy-start.1 = (bf16[2,512,512]{2,1,0:T(8,128)(2,1)}, bf16[2,512,512]{2,1,0:T(8,128)(2,1)S(1)}, u32[]{:S(2)}) copy-start(bf16[2,512,512]{2,1,0:T(8,128)(2,1)S(1)} %collective-permute-done.6.refs_2_) | copy-start | bytes 3145732
  81.1 2.3 %copy-start.4 = (bf16[4,512,256]{2,1,0:T(8,128)(2,1)}, bf16[4,512,256]{2,1,0:T(8,128)(2,1)S(1)}, u32[]{:S(2)}) copy-start(bf16[4,512,256]{2,1,0:T(8,128)(2,1)S(1)} %collective-permute-done.7.kv_first) | copy-start | bytes 3145732
  81.1 1.0 copy-start.6
  82.1 12.7 %collective-permute-start.9 = (bf16[512,512]{1,0:T(8,128)(2,1)S(1)}, bf16[512,512]{1,0:T(8,128)(2,1)S(1)}, u32[]{:S(2)}, u32[]{:S(2)}) collective-permute-start(bf16[512,512]{1,0:T(8,128)(2,1)S(1)} %slice_bitcast_fusion.1), channel_id=1, source_target_pairs={{0,16},{16,32},{32,48},{48,0},{1,17},{17,33},{33,49},{49,1},{2,18}... | collective-permute-start | bytes 1572872 | tf_op jit(solution)/shard_map/ppermute | solution.py:274
  83.4 11.4 %collective-permute-start.10 = (bf16[512,512]{1,0:T(8,128)(2,1)S(1)}, bf16[512,512]{1,0:T(8,128)(2,1)S(1)}, u32[]{:S(2)}, u32[]{:S(2)}) collective-permute-start(bf16[512,512]{1,0:T(8,128)(2,1)S(1)} %slice_bitcast_fusion), channel_id=1, source_target_pairs={{0,48},{16,0},{32,16},{48,32},{1,49},{17,1},{33,17},{49,33},{2,50}... | collective-permute-start | bytes 1572872 | tf_op jit(solution)/shard_map/ppermute | solution.py:274
  85.0 13.9 %collective-permute-start.20 = (bf16[512,512]{1,0:T(8,128)(2,1)S(1)}, bf16[512,512]{1,0:T(8,128)(2,1)S(1)}, u32[]{:S(2)}, u32[]{:S(2)}) collective-permute-start(bf16[512,512]{1,0:T(8,128)(2,1)S(1)} %copy-done.17), channel_id=1, source_target_pairs={{0,64},{64,68},{4,0},{68,4},{1,65},{65,69},{5,1},{69,5},{2,66},{66... | collective-permute-start | bytes 1572872 | tf_op jit(solution)/shard_map/ppermute | solution.py:284
  88.4 10.5 %collective-permute-start.21 = (bf16[512,512]{1,0:T(8,128)(2,1)S(1)}, bf16[512,512]{1,0:T(8,128)(2,1)S(1)}, u32[]{:S(2)}, u32[]{:S(2)}) collective-permute-start(bf16[512,512]{1,0:T(8,128)(2,1)S(1)} %copy-done.17), channel_id=1, source_target_pairs={{0,0},{64,4},{4,64},{68,68},{1,1},{65,5},{5,65},{69,69},{2,2},{66,... | collective-permute-start | bytes 1572872 | tf_op jit(solution)/shard_map/ppermute | solution.py:284
  94.8 0.8 copy-start.8
  100.8 1.2 copy-start.2
  102.0 2.2 %copy-start.3 = (bf16[4096,512]{1,0:T(8,128)(2,1)S(1)}, bf16[4096,512]{1,0:T(8,128)(2,1)}, u32[]{:S(2)}) copy-start(bf16[4096,512]{1,0:T(8,128)(2,1)} %all-gather.5.cloned.1.call-done) | copy-start | bytes 12582916
  102.0 2.5 %copy-start.5 = (bf16[4,512,256]{2,1,0:T(8,128)(2,1)S(1)}, bf16[4,512,256]{2,1,0:T(8,128)(2,1)}, u32[]{:S(2)}) copy-start(bf16[4,512,256]{2,1,0:T(8,128)(2,1)} %copy-done.4) | copy-start | bytes 3145732
  102.0 2.8 %copy-start.7 = (bf16[4,512,256]{2,1,0:T(8,128)(2,1)S(1)}, bf16[4,512,256]{2,1,0:T(8,128)(2,1)}, u32[]{:S(2)}) copy-start(bf16[4,512,256]{2,1,0:T(8,128)(2,1)} %copy-done.6) | copy-start | bytes 3145732
  104.8 1.0 copy-start.9
  113.7 6.7 %collective-permute-start.11 = (bf16[2,256,768]{2,1,0:T(8,128)(2,1)S(1)}, bf16[2,256,768]{2,1,0:T(8,128)(2,1)S(1)}, u32[]{:S(2)}, u32[]{:S(2)}) collective-permute-start(bf16[2,256,768]{2,1,0:T(8,128)(2,1)S(1)} %get-tuple-element.49), channel_id=1, source_target_pairs={{0,8},{8,0},{1,9},{9,1},{2,10},{10,2},{3,11},{11,3},{4,12},{12,4},... | collective-permute-start | bytes 2359304 | tf_op jit(solution)/shard_map/ppermute | solution.py:274
  116.1 8.1 %collective-permute-start.17 = (bf16[2,256,768]{2,1,0:T(8,128)(2,1)S(1)}, bf16[2,256,768]{2,1,0:T(8,128)(2,1)S(1)}, u32[]{:S(2)}, u32[]{:S(2)}) collective-permute-start(bf16[2,256,768]{2,1,0:T(8,128)(2,1)S(1)} %get-tuple-element.53), channel_id=1, source_target_pairs={{0,8},{8,0},{1,9},{9,1},{2,10},{10,2},{3,11},{11,3},{4,12},{12,4},... | collective-permute-start | bytes 2359304 | tf_op jit(solution)/shard_map/ppermute | solution.py:274
  116.4 7.0 %collective-permute-start.15 = (f32[4,128]{1,0:T(4,128)S(1)}, f32[4,128]{1,0:T(4,128)S(1)}, u32[]{:S(2)}, u32[]{:S(2)}) collective-permute-start(f32[4,128]{1,0:T(4,128)S(1)} %bitcast.80), channel_id=1, source_target_pairs={{0,12},{4,8},{8,4},{12,0},{1,13},{5,9},{9,5},{13,1},{2,14},{6,10},... | collective-permute-start | bytes 6152 | tf_op jit(solution)/shard_map/ppermute | solution.py:378
  120.2 4.1 %collective-permute-start.13 = (f32[4,128]{1,0:T(4,128)S(1)}, f32[4,128]{1,0:T(4,128)S(1)}, u32[]{:S(2)}, u32[]{:S(2)}) collective-permute-start(f32[4,128]{1,0:T(4,128)S(1)} %bitcast.81), channel_id=1, source_target_pairs={{0,8},{8,0},{1,9},{9,1},{2,10},{10,2},{3,11},{11,3},{4,12},{12,4},... | collective-permute-start | bytes 6152 | tf_op jit(solution)/shard_map/ppermute | solution.py:274
  120.3 4.0 %collective-permute-start.14 = (f32[4,128]{1,0:T(4,128)S(1)}, f32[4,128]{1,0:T(4,128)S(1)}, u32[]{:S(2)}, u32[]{:S(2)}) collective-permute-start(f32[4,128]{1,0:T(4,128)S(1)} %bitcast.78), channel_id=1, source_target_pairs={{0,4},{4,0},{1,5},{5,1},{2,6},{6,2},{3,7},{7,3},{8,12},{12,8},{9,1... | collective-permute-start | bytes 6152 | tf_op jit(solution)/shard_map/ppermute | solution.py:274
  120.5 12.0 %collective-permute-start.12 = (bf16[256,768]{1,0:T(8,128)(2,1)S(1)}, bf16[256,768]{1,0:T(8,128)(2,1)S(1)}, u32[]{:S(2)}, u32[]{:S(2)}) collective-permute-start(bf16[256,768]{1,0:T(8,128)(2,1)S(1)} %fusion), channel_id=1, source_target_pairs={{0,4},{4,0},{1,5},{5,1},{2,6},{6,2},{3,7},{7,3},{8,12},{12,8},{9,1... | collective-permute-start | bytes 1179656 | tf_op jit(solution)/shard_map/ppermute | solution.py:274
  132.4 10.9 %collective-permute-start.18 = (bf16[256,768]{1,0:T(8,128)(2,1)S(1)}, bf16[256,768]{1,0:T(8,128)(2,1)S(1)}, u32[]{:S(2)}, u32[]{:S(2)}) collective-permute-start(bf16[256,768]{1,0:T(8,128)(2,1)S(1)} %fusion.1), channel_id=1, source_target_pairs={{0,4},{4,0},{1,5},{5,1},{2,6},{6,2},{3,7},{7,3},{8,12},{12,8},{9,1... | collective-permute-start | bytes 1179656 | tf_op jit(solution)/shard_map/ppermute | solution.py:274
  136.0 13.0 %collective-permute-start.16 = (bf16[256,512]{1,0:T(8,128)(2,1)S(1)}, bf16[256,512]{1,0:T(8,128)(2,1)S(1)}, u32[]{:S(2)}, u32[]{:S(2)}) collective-permute-start(bf16[256,512]{1,0:T(8,128)(2,1)S(1)} %attend.2.refs_0_), channel_id=1, source_target_pairs={{0,4},{4,0},{1,5},{5,1},{2,6},{6,2},{3,7},{7,3},{8,12},{12,8},{9,1... | collective-permute-start | bytes 786440 | tf_op jit(solution)/shard_map/ppermute | solution.py:274
  144.5 9.5 %collective-permute-start.19 = (bf16[256,512]{1,0:T(8,128)(2,1)S(1)}, bf16[256,512]{1,0:T(8,128)(2,1)S(1)}, u32[]{:S(2)}, u32[]{:S(2)}) collective-permute-start(bf16[256,512]{1,0:T(8,128)(2,1)S(1)} %attend.3.refs_2_), channel_id=1, source_target_pairs={{0,4},{4,0},{1,5},{5,1},{2,6},{6,2},{3,7},{7,3},{8,12},{12,8},{9,1... | collective-permute-start | bytes 786440 | tf_op jit(solution)/shard_map/ppermute | solution.py:274
  154.0 3.4 %copy-start = (bf16[16,512,512]{2,1,0:T(8,128)(2,1)S(1)}, bf16[16,512,512]{2,1,0:T(8,128)(2,1)}, u32[]{:S(2)}) copy-start(bf16[16,512,512]{2,1,0:T(8,128)(2,1)} %all-gather.7.cloned.1.call-done) | copy-start | bytes 25165828
  159.2 12.3 %collective-permute-start.26 = (bf16[256,1024]{1,0:T(8,128)(2,1)S(1)}, bf16[256,1024]{1,0:T(8,128)(2,1)S(1)}, u32[]{:S(2)}, u32[]{:S(2)}) collective-permute-start(bf16[256,1024]{1,0:T(8,128)(2,1)S(1)} %get-tuple-element.61), channel_id=1, source_target_pairs={{0,3},{1,0},{2,1},{3,2},{4,7},{5,4},{6,5},{7,6},{8,11},{9,8},{10,9... | collective-permute-start | bytes 1572872 | tf_op jit(solution)/shard_map/ppermute | solution.py:274
  163.0 12.2 %collective-permute-start.22 = (bf16[256,1024]{1,0:T(8,128)(2,1)S(1)}, bf16[256,1024]{1,0:T(8,128)(2,1)S(1)}, u32[]{:S(2)}, u32[]{:S(2)}) collective-permute-start(bf16[256,1024]{1,0:T(8,128)(2,1)S(1)} %get-tuple-element.60), channel_id=1, source_target_pairs={{0,1},{1,2},{2,3},{3,0},{4,5},{5,6},{6,7},{7,4},{8,9},{9,10},{10,1... | collective-permute-start | bytes 1572872 | tf_op jit(solution)/shard_map/ppermute | solution.py:274
  167.0 18.8 %collective-permute-start.25 = (bf16[256,1024]{1,0:T(8,128)(2,1)S(1)}, bf16[256,1024]{1,0:T(8,128)(2,1)S(1)}, u32[]{:S(2)}, u32[]{:S(2)}) collective-permute-start(bf16[256,1024]{1,0:T(8,128)(2,1)S(1)} %get-tuple-element.67), channel_id=1, source_target_pairs={{0,1},{1,2},{2,3},{3,0},{4,5},{5,6},{6,7},{7,4},{8,9},{9,10},{10,1... | collective-permute-start | bytes 1572872 | tf_op jit(solution)/shard_map/ppermute | solution.py:274
  171.6 14.2 %collective-permute-start.27 = (bf16[256,1024]{1,0:T(8,128)(2,1)S(1)}, bf16[256,1024]{1,0:T(8,128)(2,1)S(1)}, u32[]{:S(2)}, u32[]{:S(2)}) collective-permute-start(bf16[256,1024]{1,0:T(8,128)(2,1)S(1)} %add_convert_fusion.1), channel_id=1, source_target_pairs={{0,3},{1,0},{2,1},{3,2},{4,7},{5,4},{6,5},{7,6},{8,11},{9,8},{10,9... | collective-permute-start | bytes 1572872 | tf_op jit(solution)/shard_map/ppermute | solution.py:274
  175.1 18.8 %collective-permute-start.24 = (bf16[256,1024]{1,0:T(8,128)(2,1)S(1)}, bf16[256,1024]{1,0:T(8,128)(2,1)S(1)}, u32[]{:S(2)}, u32[]{:S(2)}) collective-permute-start(bf16[256,1024]{1,0:T(8,128)(2,1)S(1)} %get-tuple-element.65), channel_id=1, source_target_pairs={{0,3},{1,0},{2,1},{3,2},{4,7},{5,4},{6,5},{7,6},{8,11},{9,8},{10,9... | collective-permute-start | bytes 1572872 | tf_op jit(solution)/shard_map/ppermute | solution.py:274
  175.4 21.6 %collective-permute-start.23 = (bf16[256,1024]{1,0:T(8,128)(2,1)S(1)}, bf16[256,1024]{1,0:T(8,128)(2,1)S(1)}, u32[]{:S(2)}, u32[]{:S(2)}) collective-permute-start(bf16[256,1024]{1,0:T(8,128)(2,1)S(1)} %add_convert_fusion.3), channel_id=1, source_target_pairs={{0,1},{1,2},{2,3},{3,0},{4,5},{5,6},{6,7},{7,4},{8,9},{9,10},{10,1... | collective-permute-start | bytes 1572872 | tf_op jit(solution)/shard_map/ppermute | solution.py:274
Sparse Core Ops, SparseCore 0:
  50.6 50.0 all-gather.4
  102.4 50.6 all-gather.6
